TPU v7x, 32 devices: a whole 2x2x4 slice. The times are simulated.
32 devices in a mesh: head: 4 (over y, x), blk: 8 (over z, core).
Axes of the slice: x: 2, y: 2, z: 4, core: 2. Of those that a mesh axis runs over, the one named last changes fastest.
Arguments:
- tokens: bfloat16 [8, 2048, 768], P(None, ('head', 'blk')), may hold values from -6 to 6
- lengths: int32 [8], replicated, may hold values from 256 to 2048, as said below
- first_gain: bfloat16 [768], P(('head', 'blk')), may hold values from 0.25 to 1.75
- first_bias: bfloat16 [768], P(('head', 'blk')), may hold values from -1.25 to 1.25
- joint_weight: bfloat16 [768, 2304], P(('head', 'blk')), may hold values from -0.21875 to 0.21875
- query_bias: bfloat16 [768], P(('head', 'blk')), may hold values from -3 to 3
- value_bias: bfloat16 [768], P(('head', 'blk')), may hold values from -0.125 to 0.125
- output_weight: bfloat16 [768, 768], P(('head', 'blk')), may hold values from -6 to 6
- output_bias: bfloat16 [768], P(('head', 'blk')), may hold values from -1.25 to 1.25
- second_gain: bfloat16 [768], P(('head', 'blk')), may hold values from 0.25 to 1.75
- second_bias: bfloat16 [768], P(('head', 'blk')), may hold values from -1.25 to 1.25
- inner_weight: bfloat16 [768, 3072], P(('head', 'blk')), may hold values from -0.21875 to 0.21875
- inner_bias: bfloat16 [3072], P(('head', 'blk')), may hold values from -1.25 to 1.25
- outer_weight: bfloat16 [3072, 768], P(('head', 'blk')), may hold values from -0.4375 to 0.4375
- outer_bias: bfloat16 [768], P(('head', 'blk')), may hold values from -3 to 3
- cotangent: bfloat16 [8, 2048, 768], P(None, ('head', 'blk')), may hold values from -6 to 6
Outputs:
- output: bfloat16 [8, 2048, 768], P(None, ('head', 'blk'))
- tokens_gradient: bfloat16 [8, 2048, 768], P(None, ('head', 'blk'))
- first_gain_gradient: float32 [768], P(('head', 'blk'))
- first_bias_gradient: float32 [768], P(('head', 'blk'))
- joint_weight_gradient: float32 [768, 2304], P(('head', 'blk'))
- query_bias_gradient: float32 [768], P(('head', 'blk'))
- value_bias_gradient: float32 [768], P(('head', 'blk'))
- output_weight_gradient: float32 [768, 768], P(('head', 'blk'))
- output_bias_gradient: float32 [768], P(('head', 'blk'))
- second_gain_gradient: float32 [768], P(('head', 'blk'))
- second_bias_gradient: float32 [768], P(('head', 'blk'))
- inner_weight_gradient: float32 [768, 3072], P(('head', 'blk'))
- inner_bias_gradient: float32 [3072], P(('head', 'blk'))
- outer_weight_gradient: float32 [3072, 768], P(('head', 'blk'))
- outer_bias_gradient: float32 [768], P(('head', 'blk'))
- stats: float32 [3], replicated
Inputs may be any that keep to these rules, and one draw needn't show every extreme that they name: `lengths`: one slot, chosen by the seed, is full (2048).
All inputs are finite; a program needn't handle non-finite values.
Results may differ from a plain program's by a relative error of at most 0.02.
Values may be sent and summed in bfloat16 or wider, within the bound.
A program may use at most 128 MiB of HBM per device.

v0:
```python
import jax
import jax.numpy as jnp
from jax import lax
from jax.experimental import pallas as pl
from jax.experimental.pallas import tpu as pltpu
from jax.sharding import PartitionSpec as P

H = 12
DH = 64


EPS = 1e-12
NEG = -1e30


def passed_along(value, axis, steps):
    count = lax.axis_size(axis)
    pairs = [(source, (source + steps) % count) for source in range(count)]
    return lax.ppermute(value, axis, pairs)


def normalize(values, gain, shift):
    average = jnp.mean(values, axis=-1, keepdims=True)
    centered = values - average
    inverse = lax.rsqrt(jnp.mean(centered * centered, axis=-1, keepdims=True) + EPS)
    normed = centered * inverse
    return (normed * gain + shift, normed, inverse)


def normalize_back(incoming, normed, inverse, gain):
    scaled = incoming * gain
    inner = (
        scaled
        - jnp.mean(scaled, axis=-1, keepdims=True)
        - normed * jnp.mean(scaled * normed, axis=-1, keepdims=True)
    )
    return (
        inner * inverse,
        jnp.sum(incoming * normed, axis=(0, 1)),
        jnp.sum(incoming, axis=(0, 1)),
    )


def gelu_exact(values):
    return jax.nn.gelu(values, approximate=False)


def key_mask(lengths, source, piece_rows, block_count, head_count):
    rows_here = jnp.arange(head_count * piece_rows, dtype=jnp.int32)
    position = (
        rows_here // piece_rows * block_count + source
    ) * piece_rows + rows_here % piece_rows
    return position[None, :] < lengths[:, None]


def attend(query_part, state, keys_block, values_block, mask):
    best, total, running = state
    scores = jnp.einsum(
        "sqhd,skhd->sqhk", query_part, keys_block, preferred_element_type=jnp.float32
    ) * DH ** (-0.5)
    scores = jnp.where(mask[:, None, None, :], scores, NEG)
    fresh = jnp.maximum(best, jnp.max(scores, axis=-1))
    decay = jnp.exp(best - fresh)
    weights = jnp.exp(scores - fresh[..., None])
    total = total * decay + jnp.sum(weights, axis=-1)
    running = running * decay[..., None] + jnp.einsum(
        "sqhk,skhd->sqhd",
        weights.astype(jnp.bfloat16),
        values_block,
        preferred_element_type=jnp.float32,
    )
    return (fresh, total, running)


def block_grads(query_part, back_part, total_part, spread_part, keys_block, values_block, mask):
    scale = DH ** (-0.5)
    scores = (
        jnp.einsum("sqhd,skhd->sqhk", query_part, keys_block, preferred_element_type=jnp.float32)
        * scale
    )
    scores = jnp.where(mask[:, None, None, :], scores, NEG)
    chances = jnp.exp(scores - total_part[..., None])
    back_chances = jnp.einsum(
        "sqhd,skhd->sqhk", back_part, values_block, preferred_element_type=jnp.float32
    )
    back_scores = (chances * (back_chances - spread_part[..., None])).astype(jnp.bfloat16)
    query_step = (
        jnp.einsum("sqhk,skhd->sqhd", back_scores, keys_block, preferred_element_type=jnp.float32)
        * scale
    )
    key_step = (
        jnp.einsum("sqhk,sqhd->skhd", back_scores, query_part, preferred_element_type=jnp.float32)
        * scale
    )
    value_step = jnp.einsum(
        "sqhk,sqhd->skhd",
        chances.astype(jnp.bfloat16),
        back_part,
        preferred_element_type=jnp.float32,
    )
    return (query_step, key_step, value_step)


def on_device(
    tokens,
    lengths,
    first_gain,
    first_bias,
    joint_weight,
    query_bias,
    value_bias,
    output_weight,
    output_bias,
    second_gain,
    second_bias,
    inner_weight,
    inner_bias,
    outer_weight,
    outer_bias,
    cotangent,
):
    head_count = lax.axis_size("head")
    block_count = lax.axis_size("blk")
    block = lax.axis_index("blk")
    quarter = lax.axis_index("head")
    (
        gain_one,
        shift_one,
        joint_full,
        query_shift,
        value_shift,
        output_full,
        output_shift,
        gain_two,
        shift_two,
        inner_full,
        inner_shift,
        outer_full,
        outer_shift,
    ) = (
        lax.all_gather(first_gain, ("head", "blk"), axis=0, tiled=True),
        lax.all_gather(first_bias, ("head", "blk"), axis=0, tiled=True),
        lax.all_gather(joint_weight, ("head", "blk"), axis=0, tiled=True),
        lax.all_gather(query_bias, ("head", "blk"), axis=0, tiled=True),
        lax.all_gather(value_bias, ("head", "blk"), axis=0, tiled=True),
        lax.all_gather(output_weight, ("head", "blk"), axis=0, tiled=True),
        lax.all_gather(output_bias, ("head", "blk"), axis=0, tiled=True),
        lax.all_gather(second_gain, ("head", "blk"), axis=0, tiled=True),
        lax.all_gather(second_bias, ("head", "blk"), axis=0, tiled=True),
        lax.all_gather(inner_weight, ("head", "blk"), axis=0, tiled=True),
        lax.all_gather(inner_bias, ("head", "blk"), axis=0, tiled=True),
        lax.all_gather(outer_weight, ("head", "blk"), axis=0, tiled=True),
        lax.all_gather(outer_bias, ("head", "blk"), axis=0, tiled=True),
    )
    sequences, piece_rows, width = tokens.shape
    heads_here = H // head_count
    head_width = heads_here * DH
    rows = head_count * piece_rows
    shape_heads = (sequences, rows, heads_here, DH)
    shape_flat = (sequences, rows, head_width)
    own_position = (quarter * block_count + block) * piece_rows + jnp.arange(
        piece_rows, dtype=jnp.int32
    )
    valid = own_position[None, :] < lengths[:, None]
    keep = valid[..., None]
    inputs = tokens.astype(jnp.float32)
    gain_one_wide = gain_one.astype(jnp.float32)
    gain_two_wide = gain_two.astype(jnp.float32)
    first_out, first_unit, first_scale = normalize(
        inputs, gain_one_wide, shift_one.astype(jnp.float32)
    )
    first_low = first_out.astype(jnp.bfloat16)
    joint = jnp.einsum("scd,de->sce", first_low, joint_full, preferred_element_type=jnp.float32)
    query_flat = (joint[..., :width] + query_shift.astype(jnp.float32)).astype(jnp.bfloat16)
    key_flat = joint[..., width : 2 * width].astype(jnp.bfloat16)
    value_flat = (joint[..., 2 * width :] + value_shift.astype(jnp.float32)).astype(jnp.bfloat16)
    query_flat, key_flat, value_flat = (
        lax.all_to_all(query_flat, "head", split_axis=2, concat_axis=1, tiled=True),
        lax.all_to_all(key_flat, "head", split_axis=2, concat_axis=1, tiled=True),
        lax.all_to_all(value_flat, "head", split_axis=2, concat_axis=1, tiled=True),
    )
    query_rows = query_flat.reshape(shape_heads)
    key_rows = key_flat.reshape(shape_heads)
    value_rows = value_flat.reshape(shape_heads)

    def visit(carry):
        keys_block, values_block, source, state = carry
        keys_block, values_block = passed_along((keys_block, values_block), "blk", 1)
        source = (source - 1) % block_count
        mask = key_mask(lengths, source, piece_rows, block_count, head_count)
        return (
            keys_block,
            values_block,
            source,
            attend(query_rows, state, keys_block, values_block, mask),
        )

    start_state = (
        jnp.full((sequences, rows, heads_here), NEG, jnp.float32),
        jnp.zeros((sequences, rows, heads_here), jnp.float32),
        jnp.zeros(shape_heads, jnp.float32),
    )
    first_state = attend(
        query_rows,
        start_state,
        key_rows,
        value_rows,
        key_mask(lengths, block, piece_rows, block_count, head_count),
    )
    carry = (key_rows, value_rows, block, first_state)
    carry = lax.fori_loop(0, block_count // 2 - 1, lambda turn, state: visit(visit(state)), carry)
    best, total, running = visit(carry)[3]
    context = running / total[..., None]
    log_total = best + jnp.log(total)
    context_low = context.astype(jnp.bfloat16).reshape(shape_flat)
    context_tokens = lax.all_to_all(context_low, "head", split_axis=1, concat_axis=2, tiled=True)
    branch = jnp.einsum(
        "sce,ed->scd", context_tokens, output_full, preferred_element_type=jnp.float32
    ) + output_shift.astype(jnp.float32)
    residual = inputs + branch
    second_out, second_unit, second_scale = normalize(
        residual, gain_two_wide, shift_two.astype(jnp.float32)
    )
    second_low = second_out.astype(jnp.bfloat16)
    inner = jnp.einsum(
        "scd,df->scf", second_low, inner_full, preferred_element_type=jnp.float32
    ) + inner_shift.astype(jnp.float32)
    activated = gelu_exact(inner).astype(jnp.bfloat16)
    feed = jnp.einsum(
        "scf,fd->scd", activated, outer_full, preferred_element_type=jnp.float32
    ) + outer_shift.astype(jnp.float32)
    result = residual + feed
    output = jnp.where(keep, result, 0.0).astype(jnp.bfloat16)
    sums = lax.psum(
        (
            jnp.sum(jnp.where(keep, result * result, 0.0)),
            jnp.sum(jnp.where(keep, branch * branch, 0.0)),
            jnp.sum(jnp.where(keep, feed * feed, 0.0)),
        ),
        ("head", "blk"),
    )
    count = jnp.sum(lengths).astype(jnp.float32) * width
    stats = jnp.sqrt(jnp.stack(sums) / count + 1e-06)
    back_result = jnp.where(keep, cotangent.astype(jnp.float32), 0.0)
    back_feed = back_result.astype(jnp.bfloat16)
    outer_gradient = jnp.einsum(
        "scf,scd->fd", activated, back_feed, preferred_element_type=jnp.float32
    )
    outer_shift_gradient = jnp.sum(back_feed.astype(jnp.float32), axis=(0, 1))
    back_active = jnp.einsum(
        "scd,fd->scf", back_feed, outer_full, preferred_element_type=jnp.float32
    )
    back_inner = jax.vjp(gelu_exact, inner)[1](back_active)[0].astype(jnp.bfloat16)
    inner_gradient = jnp.einsum(
        "scd,scf->df", second_low, back_inner, preferred_element_type=jnp.float32
    )
    inner_shift_gradient = jnp.sum(back_inner.astype(jnp.float32), axis=(0, 1))
    back_second = jnp.einsum(
        "scf,df->scd", back_inner, inner_full, preferred_element_type=jnp.float32
    )
    back_norm_two, gain_two_gradient, shift_two_gradient = normalize_back(
        back_second, second_unit, second_scale, gain_two_wide
    )
    back_residual = back_result + back_norm_two
    back_branch = back_residual.astype(jnp.bfloat16)
    output_gradient = jnp.einsum(
        "sce,scd->ed", context_tokens, back_branch, preferred_element_type=jnp.float32
    )
    output_shift_gradient = jnp.sum(back_branch.astype(jnp.float32), axis=(0, 1))
    back_context = jnp.einsum(
        "scd,ed->sce", back_branch, output_full, preferred_element_type=jnp.float32
    ).astype(jnp.bfloat16)
    back_context = lax.all_to_all(back_context, "head", split_axis=2, concat_axis=1, tiled=True)
    back_heads = back_context.reshape(shape_heads)
    spread = jnp.sum(back_heads.astype(jnp.float32) * context, axis=-1)
    zero_heads = jnp.zeros(shape_heads, jnp.float32)

    def pass_keys(carry):
        keys_block, values_block, key_sum, value_sum, query_sum, source = carry
        mask = key_mask(lengths, source, piece_rows, block_count, head_count)
        query_step, key_step, value_step = block_grads(
            query_rows, back_heads, log_total, spread, keys_block, values_block, mask
        )
        keys_block, values_block = passed_along((keys_block, values_block), "blk", 1)
        key_sum, value_sum = passed_along((key_sum + key_step, value_sum + value_step), "blk", 1)
        return (
            keys_block,
            values_block,
            key_sum,
            value_sum,
            query_sum + query_step,
            (source - 1) % block_count,
        )

    carry = (key_rows, value_rows, zero_heads, zero_heads, zero_heads, block)
    carry = lax.fori_loop(
        0, block_count // 2, lambda turn, state: pass_keys(pass_keys(state)), carry
    )
    key_sum, value_sum, query_sum = (carry[2], carry[3], carry[4])
    back_query, back_key, back_value = (
        lax.all_to_all(
            query_sum.astype(jnp.bfloat16).reshape(shape_flat),
            "head",
            split_axis=1,
            concat_axis=2,
            tiled=True,
        ),
        lax.all_to_all(
            key_sum.astype(jnp.bfloat16).reshape(shape_flat),
            "head",
            split_axis=1,
            concat_axis=2,
            tiled=True,
        ),
        lax.all_to_all(
            value_sum.astype(jnp.bfloat16).reshape(shape_flat),
            "head",
            split_axis=1,
            concat_axis=2,
            tiled=True,
        ),
    )
    back_joint = jnp.concatenate([back_query, back_key, back_value], axis=-1)
    joint_gradient = jnp.einsum(
        "scd,sce->de", first_low, back_joint, preferred_element_type=jnp.float32
    )
    query_shift_gradient = jnp.sum(back_query.astype(jnp.float32), axis=(0, 1))
    value_shift_gradient = jnp.sum(back_value.astype(jnp.float32), axis=(0, 1))
    back_first = jnp.einsum(
        "sce,de->scd", back_joint, joint_full, preferred_element_type=jnp.float32
    )
    back_norm_one, gain_one_gradient, shift_one_gradient = normalize_back(
        back_first, first_unit, first_scale, gain_one_wide
    )
    tokens_gradient = (back_residual + back_norm_one).astype(jnp.bfloat16)
    shards = (
        lax.psum_scatter(gain_one_gradient, ("head", "blk"), scatter_dimension=0, tiled=True),
        lax.psum_scatter(shift_one_gradient, ("head", "blk"), scatter_dimension=0, tiled=True),
        lax.psum_scatter(joint_gradient, ("head", "blk"), scatter_dimension=0, tiled=True),
        lax.psum_scatter(query_shift_gradient, ("head", "blk"), scatter_dimension=0, tiled=True),
        lax.psum_scatter(value_shift_gradient, ("head", "blk"), scatter_dimension=0, tiled=True),
        lax.psum_scatter(output_gradient, ("head", "blk"), scatter_dimension=0, tiled=True),
        lax.psum_scatter(output_shift_gradient, ("head", "blk"), scatter_dimension=0, tiled=True),
        lax.psum_scatter(gain_two_gradient, ("head", "blk"), scatter_dimension=0, tiled=True),
        lax.psum_scatter(shift_two_gradient, ("head", "blk"), scatter_dimension=0, tiled=True),
        lax.psum_scatter(inner_gradient, ("head", "blk"), scatter_dimension=0, tiled=True),
        lax.psum_scatter(inner_shift_gradient, ("head", "blk"), scatter_dimension=0, tiled=True),
        lax.psum_scatter(outer_gradient, ("head", "blk"), scatter_dimension=0, tiled=True),
        lax.psum_scatter(outer_shift_gradient, ("head", "blk"), scatter_dimension=0, tiled=True),
    )
    return (
        output,
        tokens_gradient,
        shards[0],
        shards[1],
        shards[2],
        shards[3],
        shards[4],
        shards[5],
        shards[6],
        shards[7],
        shards[8],
        shards[9],
        shards[10],
        shards[11],
        shards[12],
        stats,
    )


MESH = pl.DeviceIdType.MESH
WIDTH = H * DH
GROUP = 3 * DH
NT = (((1,), (1,)), ((), ()))
NN = (((1,), (0,)), ((), ()))


def place():
    head = lax.axis_index("head")
    blk = lax.axis_index("blk")
    return head // 2, lax.rem(head, 2), blk // 2, lax.rem(blk, 2)


def at(y, x, z, c):
    return (y * 2 + x, z * 2 + c)


def number(y, x, z, c):
    return y * 16 + x * 8 + z * 2 + c


def column(t):
    return t // 4, lax.rem(t, 4)


def meet(peers):
    barrier = pltpu.get_barrier_semaphore()
    for peer in peers:
        pl.semaphore_signal(barrier, inc=1, device_id=peer, device_id_type=MESH)
    pl.semaphore_wait(barrier, len(peers))


class Mover:
    def __init__(self, send_sem, local_sem, anyone):
        self.send_sem = send_sem
        self.local_sem = local_sem
        self.anyone = anyone
        self.zero = anyone[0] * 0
        self.sent = []
        self.local = []

    def push(self, source, target, sem, device):
        self.push_made(lambda: (source, target, sem), device)

    def push_made(self, make, device):
        spot = len(self.sent)
        self.sent.append((make, spot, device))
        self.copy(make, spot, device).start()

    def copy(self, make, spot, device):
        source, target, sem = make()
        return remote(source, target, self.send_sem.at[self.zero + spot], sem, device)

    def keep(self, source, target):
        parts = (source, target, self.local_sem.at[len(self.local)])
        pltpu.make_async_copy(*parts).start()
        self.local.append(parts)
        return len(self.local) - 1

    def kept(self, spot):
        pltpu.make_async_copy(*self.local[spot]).wait()

    def landed(self, target, sem):
        remote(target, target, self.send_sem.at[self.zero], sem, self.anyone).wait_recv()

    def finish(self, kept=()):
        for parts in self.sent:
            self.copy(*parts).wait_send()
        for spot in kept:
            self.kept(spot)


def remote(source, target, send_sem, recv_sem, device):
    return pltpu.make_async_remote_copy(
        src_ref=source,
        dst_ref=target,
        send_sem=send_sem,
        recv_sem=recv_sem,
        device_id=device,
        device_id_type=MESH,
    )


def unpack(small_all, vectors):
    for block in range(32):
        tile = wide(small_all[block])
        vectors[:, block * 24 : block * 24 + 24] = tile[:8, :24]


def forward_kernel(
    length, tokens, cotangent, wj, wo, wi, wu, small,
    first_low, query, key, value, context, context_rows, cot_own, tok_own, wo_all, wi_all, wu_all, small_all, wj_flat,
    send_sem, local_sem, tok_sem, cot_sem, weight_sem, small_sem, wja_sem, wjb_sem, wjc_sem, ctx_send, ctx_recv,
    ctx_local, tok_all, wj_all, vectors, turned, mixed_low,
):
    y, x, z, c = place()
    mine = number(y, x, z, c)
    quarter = x * 2 + c
    spot = y * 4 + z
    other_core = at(y, x, z, 1 - c)
    across = at(y, 1 - x, z, c)
    diagonal = at(y, 1 - x, z, 1 - c)
    down = at(1 - y, x, z, c)
    y1, x1 = jnp.where(c == 0, y, 1 - y), jnp.where(c == 0, 1 - x, x)
    y2, x2 = jnp.where(c == 0, 1 - y, y), jnp.where(c == 0, x, 1 - x)
    first, second = at(y1, x1, z, c), at(y2, x2, z, c)
    spots = [column(lax.rem(spot + k, 8)) for k in range(1, 8)]
    back_spots = [column(lax.rem(spot + 8 - k, 8)) for k in range(1, 8)]
    lines = [lax.rem(z + 4 - k, 4) for k in range(4)]
    ahead = [at(y, x, lax.rem(z + k, 4), c) for k in range(1, 4)]
    line_blocks = [number(y, x, zz, c) for zz in lines]
    first_blocks = [number(y1, x1, zz, c) for zz in lines]
    second_blocks = [number(yy, xx, zz, c) for yy, xx in ((y2, x2), (1 - y, 1 - x)) for zz in lines]
    core_blocks = [number(yy, xx, zz, 1 - c) for yy in range(2) for xx in range(2) for zz in range(4)]
    group = quad(x, c)
    meet([at(yy, x, zz, c) for yy, zz in spots] + [across, other_core, diagonal])
    move = Mover(send_sem, local_sem, other_core)
    sources = (wo, wi, wu)
    wholes = (wo_all, wi_all, wu_all)

    for yy, zz in spots:
        move.push(tokens.at[yy * 4 + zz], tok_all.at[mine], tok_sem.at[mine], at(yy, x, zz, c))
    for xx, cc in group:
        move.push(wj.at[xx * 2 + cc], wj_all.at[y, x, z, c], wja_sem.at[quarter], at(y, xx, z, cc))
    move.keep(wj.at[quarter], wj_all.at[y, x, z, c])
    move.push(tokens.at[spot], tok_all.at[mine], tok_sem.at[mine], across)
    move.push(tokens.at[spot], tok_all.at[mine], tok_sem.at[mine], other_core)
    move.keep(tokens.at[spot], tok_all.at[mine])
    for device in ahead + [first, second, other_core]:
        move.push(small, small_all.at[mine], small_sem.at[mine], device)
    move.keep(small, small_all.at[mine])

    def hand(block, own, device):
        for i in range(3):
            move.push_made(
                lambda i=i: (
                    sources[i] if own else wholes[i].at[block],
                    wholes[i].at[block],
                    weight_sem.at[move.zero + i, block],
                ),
                device,
            )

    def arrive(block):
        for i in range(3):
            move.landed(wholes[i].at[block], weight_sem.at[i, block])

    def pass_small(blocks, devices):
        for block in blocks:
            move.landed(small_all.at[block], small_sem.at[block])
            for device in devices:
                move.push(small_all.at[block], small_all.at[block], small_sem.at[block], device)

    for device in ahead:
        hand(mine, True, device)
    for source, whole in zip(sources, wholes):
        move.keep(source, whole.at[mine])
    hand(mine, True, first)
    hand(mine, True, second)
    hand(mine, True, other_core)

    for xx, cc in group:
        move.landed(wj_all.at[y, xx, z, cc], wja_sem.at[xx * 2 + cc])
    move.kept(0)
    for device in ahead:
        move.push(wj_all.at[y, :, z], wj_all.at[y, :, z], wjb_sem.at[z], device)
    move.push(wj_all.at[y, :, z], wj_all.at[y, :, z], wjc_sem.at[z], down)
    pass_small(line_blocks[1:], (first, second, other_core))
    for yy, zz in back_spots:
        block = number(yy, x, zz, c)
        move.landed(tok_all.at[block], tok_sem.at[block])
        move.push(tok_all.at[block], tok_all.at[block], tok_sem.at[block], across)
        move.push(tok_all.at[block], tok_all.at[block], tok_sem.at[block], other_core)
    for zz in lines[1:]:
        move.landed(wj_all.at[y, :, zz], wjb_sem.at[zz])
        move.push(wj_all.at[y, :, zz], wj_all.at[y, :, zz], wjc_sem.at[zz], down)
    for yy, zz in spots:
        move.push(cotangent.at[yy * 4 + zz], cot_own.at[spot], cot_sem.at[spot], at(yy, x, zz, c))
    move.keep(cotangent.at[spot], cot_own.at[spot])
    pass_small(first_blocks, (second, other_core))
    pass_small(second_blocks, (other_core,))
    for yy, zz in [(y, z)] + back_spots:
        block = number(yy, 1 - x, zz, c)
        move.landed(tok_all.at[block], tok_sem.at[block])
        move.push(tok_all.at[block], tok_all.at[block], tok_sem.at[block], other_core)
    for block in line_blocks[1:]:
        arrive(block)
        hand(block, False, first)
        hand(block, False, second)
        hand(block, False, other_core)
    for block in core_blocks:
        move.landed(small_all.at[block], small_sem.at[block])
    for zz in lines:
        move.landed(wj_all.at[1 - y, :, zz], wjc_sem.at[zz])
    for yy, zz in [(y, z)] + back_spots:
        for xx in (x, 1 - x):
            block = number(yy, xx, zz, 1 - c)
            move.landed(tok_all.at[block], tok_sem.at[block])
    move.kept(1)
    move.kept(2)

    unpack(small_all, vectors)
    rows = query.shape[1]
    for yy in range(2):
        for xx in range(2):
            for zz in range(4):
                pair = jnp.concatenate([wide(wj_all[yy, xx, zz, cc]) for cc in range(2)], axis=0)
                row = number(yy, xx, zz, 0) * 24
                wj_flat[row : row + 48, :] = pair.astype(jnp.bfloat16)
    lane = lax.broadcasted_iota(jnp.int32, (ROWS, DH), 1)
    row_at = lax.broadcasted_iota(jnp.int32, (ROWS, DH), 0)
    one_lane = jnp.where(lane == 0, 1.0, 0.0).astype(jnp.bfloat16)
    three_lanes = jnp.where(lane < 3, 1.0, 0.0).astype(jnp.bfloat16)
    gain, shift = vectors[0:1, :], vectors[1:2, :]
    query_all, value_all = vectors[2:3, :], vectors[3:4, :]

    def chosen(whole):
        total = jnp.zeros((1, GROUP), jnp.float32)
        for q in range(4):
            total = jnp.where(quarter == q, whole[:, q * GROUP : (q + 1) * GROUP], total)
        return total

    query_shift, value_shift = chosen(query_all), chosen(value_all)
    blocks = ROWS // tokens.shape[1]

    def project(i, _):
        here = pl.ds(i * ROWS, ROWS)
        raw = tok_all[pl.ds(i * blocks, blocks)].reshape(ROWS, WIDTH)
        normed = normalize(wide(raw), gain, shift)[0].astype(jnp.bfloat16)
        first_low[here, :] = normed
        joint = dot(normed, wj_flat[...])
        low_q = ((joint[:, :GROUP] + query_shift).astype(jnp.bfloat16) * DH ** (-0.5)).astype(jnp.bfloat16)
        low_k = joint[:, GROUP : 2 * GROUP].astype(jnp.bfloat16)
        low_v = (joint[:, 2 * GROUP :] + value_shift).astype(jnp.bfloat16)
        mask = jnp.where(row_at + i * ROWS < length[0], 0.0, NEG)
        key_side = jnp.where(lane == 0, mask, jnp.where(lane < 4, 1.0, 0.0)).astype(jnp.bfloat16)
        for h in range(3):
            here_h = slice(h * DH, (h + 1) * DH)
            query[h, here, :] = jnp.concatenate([low_q[:, here_h], one_lane], axis=1)
            key[h, here, :] = jnp.concatenate([low_k[:, here_h], key_side], axis=1)
            value[h, here, :] = jnp.concatenate([low_v[:, here_h], three_lanes], axis=1)
        return 0

    lax.fori_loop(0, rows // ROWS, project, 0)
    eye = jnp.eye(72, 2 * DH, dtype=jnp.bfloat16)
    for h in range(3):
        turned[h] = dot(eye, value[h], NT).astype(jnp.bfloat16)
    side = lax.broadcasted_iota(jnp.int32, (DH, ROWS), 0)

    def ctx_piece(j, cc):
        yy, xx, zz = j // 4, lax.rem(j // 2, 2), pl.ds(lax.rem(j, 2) * 2, 2)
        return mixed_low.at[yy, xx, zz, cc], context_rows.at[quarter, yy, zz]

    def block(j, _):
        here = pl.ds(j * ROWS, ROWS)
        whole = []
        for h in range(3):
            scores = dot(key[h], query[h, here, :], NT)
            best = jnp.max(scores, axis=0, keepdims=True)
            weights = jnp.exp(scores - best).astype(jnp.bfloat16)
            mixed = dot(turned[h], weights)
            total = mixed[DH : DH + 1, :]
            mixed = mixed[:DH, :] / total
            log_total = best + jnp.log(total)
            high = log_total.astype(jnp.bfloat16).astype(jnp.float32)
            middle = (log_total - high).astype(jnp.bfloat16).astype(jnp.float32)
            low = log_total - high - middle
            extra = jnp.where(
                side == 0, 1.0, jnp.where(side == 1, -high, jnp.where(side == 2, -middle, jnp.where(side == 3, -low, 0.0)))
            )
            straight = jnp.concatenate([mixed, extra], axis=0).T
            query[h, here, DH:] = straight[:, DH:].astype(jnp.bfloat16)
            whole.append(straight[:, :DH])
        mixed = jnp.concatenate(whole, axis=1)
        yy, xx, zz = j // 4, lax.rem(j // 2, 2), lax.rem(j, 2) * 2
        low = mixed.astype(jnp.bfloat16)
        context[here, :] = low
        piece = tokens.shape[1]
        for k in range(2):
            for cc in range(2):
                start = (k * 2 + cc) * piece
                mixed_low[yy, xx, zz + k, cc] = low[start : start + piece]
        for cc in range(2):
            source, target = ctx_piece(j, cc)

            @pl.when(jnp.logical_and(xx == x, c == cc))
            def _():
                pltpu.make_async_copy(source, target, ctx_local.at[j]).start()

            @pl.when(jnp.logical_not(jnp.logical_and(xx == x, c == cc)))
            def _():
                remote(source, target, ctx_send.at[j, cc], ctx_recv.at[quarter, j], at(y, xx, z, cc)).start()

        @pl.when(j == 2)
        def _():
            for b in first_blocks:
                arrive(b)
                hand(b, False, second)
                hand(b, False, other_core)

        @pl.when(j == 6)
        def _():
            for b in second_blocks:
                arrive(b)
                hand(b, False, other_core)

        return 0

    lax.fori_loop(0, rows // ROWS, block, 0)
    for yy, zz in back_spots:
        move.landed(cot_own.at[yy * 4 + zz], cot_sem.at[yy * 4 + zz])
    for b in core_blocks:
        arrive(b)
    tok_copies = []
    for i in range(8):
        yy, zz = i // 4, i % 4
        tok_copies.append(pltpu.make_async_copy(tok_all.at[number(yy, x, zz, c)], tok_own.at[i], local_sem.at[8 + i]))
        tok_copies[-1].start()

    def settle(j, _):
        xx = lax.rem(j // 2, 2)
        for cc in range(2):
            source, target = ctx_piece(j, cc)

            @pl.when(jnp.logical_and(xx == x, c == cc))
            def _():
                pltpu.make_async_copy(source, target, ctx_local.at[j]).wait()

            @pl.when(jnp.logical_not(jnp.logical_and(xx == x, c == cc)))
            def _():
                remote(source, target, ctx_send.at[j, cc], ctx_recv.at[quarter, j], at(y, xx, z, cc)).wait_send()

        return 0

    lax.fori_loop(0, rows // ROWS, settle, 0)
    for xx, cc in group:
        for yy in range(2):
            for half in range(2):
                j = yy * 4 + x * 2 + half
                target = context_rows.at[xx * 2 + cc, yy, pl.ds(half * 2, 2)]
                move.landed(target, ctx_recv.at[xx * 2 + cc, j])
    move.finish(range(3, len(move.local)))
    for copy in tok_copies:
        copy.wait()


def comm_call(kernel, outs, args, sends, locals_, sems, scratch, ident, space=None):
    space = space or [pltpu.HBM] * len(args)
    return pl.pallas_call(
        kernel,
        out_shape=[jax.ShapeDtypeStruct(shape, dtype) for shape, dtype, _ in outs],
        in_specs=[pl.BlockSpec(memory_space=one) for one in space],
        out_specs=[pl.BlockSpec(memory_space=one) for _, _, one in outs],
        scratch_shapes=[
            pltpu.SemaphoreType.DMA((sends,)),
            pltpu.SemaphoreType.DMA((max(locals_, 1),)),
            *[pltpu.SemaphoreType.DMA(shape) for shape in sems],
            *scratch,
        ],
        compiler_params=pltpu.CompilerParams(
            collective_id=ident, has_side_effects=True, vmem_limit_bytes=61 * 1024 * 1024
        ),
    )(*args)


def quad(x, c):
    return [(lax.rem(x + dx, 2), lax.rem(c + dc, 2)) for dx, dc in ((0, 1), (1, 0), (1, 1))]


def wide(value):
    return value.astype(jnp.float32)


def dot(a, b, dims=NN):
    return lax.dot_general(a, b, dims, preferred_element_type=jnp.float32)


ROWS = 256


TN = (((0,), (0,)), ((), ()))
BACK_ROWS = 512
KEY_ROWS = 1024


def three(value):
    high = value.astype(jnp.bfloat16).astype(jnp.float32)
    middle = (value - high).astype(jnp.bfloat16).astype(jnp.float32)
    return high, middle, value - high - middle


def mean_of(value):
    return jnp.mean(value, axis=-1, keepdims=True)


TN = (((0,), (0,)), ((), ()))
BACK_ROWS = 512
KEY_ROWS = 1024


def three(value):
    high = value.astype(jnp.bfloat16).astype(jnp.float32)
    middle = (value - high).astype(jnp.bfloat16).astype(jnp.float32)
    return high, middle, value - high - middle


def mean_of(value):
    return jnp.mean(value, axis=-1, keepdims=True)


def feed_kernel(
    length, context_rows, tok_own, cot_own, wo, small_all, wi_far, wu_far,
    gu_far, gi_far, go_far, gs_far, output, back_context, back_residual,
    send_sem, local_sem, sem_out, sem_back,
    gu, gi, go, gs, wi, back_near, vectors, inner_shift, active, back_inner, output_low,
):
    bf16, f32 = jnp.bfloat16, jnp.float32
    y, x, z, c = place()
    spot = y * 4 + z
    mine = x * 2 + c
    other_core = at(y, x, z, 1 - c)
    across = at(y, 1 - x, z, c)
    diagonal = at(y, 1 - x, z, 1 - c)
    spots = [column(lax.rem(spot + k, 8)) for k in range(1, 8)]
    group = quad(x, c)
    meet([at(yy, x, zz, c) for yy, zz in spots] + [across, other_core, diagonal])
    move = Mover(send_sem, local_sem, other_core)
    width = wo.shape[0]
    ff = wi.shape[1]
    move.keep(wi_far, wi)
    move.keep(wu_far, gu)

    piece = tok_own.shape[1]
    rows = tok_own.shape[0] * piece
    steps = ff // width
    unpack(small_all, vectors)
    ff_piece = ff // 32
    for block in range(32):
        inner_shift[:, block * ff_piece : (block + 1) * ff_piece] = wide(small_all[block])[8:9, :ff_piece]

    spot_at = lax.broadcasted_iota(jnp.int32, (8, piece, 1), 0)
    position = number(spot_at // 4, x, lax.rem(spot_at, 4), c) * piece
    position = position + lax.broadcasted_iota(jnp.int32, (8, piece, 1), 1)
    keep = jnp.where(position < length[0], 1.0, 0.0).reshape(rows, 1) > 0.5

    def column_sum(item):
        return jnp.sum(item, axis=0, keepdims=True)

    def square(item):
        return jnp.sum(item * item)

    branch = vectors[4:5, :] + dot(context_rows[0].reshape(rows, GROUP), wo[:GROUP, :])
    for g in range(1, 4):
        branch = branch + dot(context_rows[g].reshape(rows, GROUP), wo[g * GROUP : (g + 1) * GROUP, :])
    residual = wide(tok_own[...].reshape(rows, width)) + branch
    branch_total = square(jnp.where(keep, branch, 0.0))
    average = mean_of(residual)
    centered = residual - average
    inverse = lax.rsqrt(mean_of(centered * centered) + EPS)
    unit = centered * inverse
    second_low = (unit * vectors[5:6, :] + vectors[6:7, :]).astype(bf16)
    back_result = jnp.where(keep, wide(cot_own[...].reshape(rows, width)), 0.0)
    back_feed = back_result.astype(bf16)
    move.kept(0)
    move.kept(1)

    def middle(step, sums_here):
        back_second, feed = sums_here
        cols = pl.ds(pl.multiple_of(step * width, width), width)
        wi_here = wi[:, cols]
        inner = dot(second_low, wi_here) + inner_shift[:, cols]
        chance = 0.5 * (1.0 + lax.erf(inner * 0.7071067811865476))
        low = (inner * chance).astype(bf16)
        active[:, cols] = low
        wu_here = gu[step].reshape(width, width)
        slope = chance + inner * jnp.exp(inner * inner * -0.5) * 0.3989422804014327
        back = (dot(back_feed, wu_here, NT) * slope).astype(bf16)
        back_inner[:, cols] = back
        return back_second + dot(back, wi_here, NT), feed + dot(low, wu_here)

    zero = jnp.zeros((rows, width), f32)
    back_second, feed = lax.fori_loop(0, steps, middle, (zero, zero))
    scaled = back_second * vectors[5:6, :]
    back_res = back_result + inverse * (scaled - mean_of(scaled) - unit * mean_of(scaled * unit))
    back_residual[...] = back_res
    back_branch = back_res.astype(bf16)
    short = jnp.concatenate(
        [
            column_sum(wide(back_feed)), column_sum(back_second * unit), column_sum(back_second),
            column_sum(wide(back_branch)), jnp.zeros((4, width), f32),
        ],
        axis=0,
    )
    for g in range(4):
        back_near[g] = dot(back_branch, wo[g * GROUP : (g + 1) * GROUP, :], NT).astype(bf16).reshape(8, piece, GROUP)
    for xx, cc in group[::-1]:
        for yy in range(2):
            move.push(
                back_near.at[xx * 2 + cc, pl.ds(yy * 4, 4)],
                back_context.at[yy, x, :, c],
                sem_back.at[mine, yy],
                at(y, xx, z, cc),
            )
    for yy in range(2):
        move.keep(back_near.at[mine, pl.ds(yy * 4, 4)], back_context.at[yy, x, :, c])

    feed = feed + vectors[7:8, :]
    result = jnp.where(keep, residual + feed, 0.0)
    output_low[...] = result.astype(bf16).reshape(8, piece, width)
    for yy, zz in spots:
        move.push(output_low.at[yy * 4 + zz], output.at[spot], sem_out.at[spot], at(yy, x, zz, c))
    move.keep(output_low.at[spot], output.at[spot])

    totals = (square(result), branch_total, square(jnp.where(keep, feed, 0.0)))
    lane = lax.broadcasted_iota(jnp.int32, (1, 128), 1)
    stat_row = jnp.where(lane == 0, totals[0], jnp.where(lane == 1, totals[1], jnp.where(lane == 2, totals[2], 0.0)))
    lead = width // 32
    wide_piece = ff // 32
    for step in range(steps):
        grad = dot(active[:, step * width : (step + 1) * width], back_feed, TN).astype(bf16)
        for zz in range(4):
            for cc in range(2):
                row = (zz * 2 + cc) * wide_piece
                gu[step, zz, cc] = grad[row : row + wide_piece, :]
        move.keep(gu.at[step], gu_far.at[step])
    for step in range(steps):
        grad = dot(second_low, back_inner[:, step * width : (step + 1) * width], TN)
        for block in range(32):
            gi[block // 8, block % 8 // 2, block % 2, :, step * width : (step + 1) * width] = grad[
                block * lead : (block + 1) * lead, :
            ].astype(bf16)
    move.keep(gi, gi_far)
    for g in range(4):
        grad = dot(context_rows[g].reshape(rows, GROUP), back_branch, TN)
        for zz in range(4):
            for cc in range(2):
                row = (zz * 2 + cc) * lead
                go[g, zz, cc] = grad[row : row + lead, :].astype(bf16)
        move.keep(go.at[g], go_far.at[g])

    long = column_sum(wide(back_inner[...]))
    for block in range(32):
        at_block = (block // 8, block % 8 // 2, block % 2)
        gs[at_block] = jnp.zeros((8, 128), f32)
        gs[at_block + (slice(0, 8), slice(0, lead))] = short[:, block * lead : (block + 1) * lead]
        gs[at_block + (slice(4, 5), slice(0, wide_piece))] = long[:, block * wide_piece : (block + 1) * wide_piece]
        gs[at_block + (slice(5, 6), slice(None))] = stat_row
    move.keep(gs, gs_far)
    for xx, cc in group:
        for yy in range(2):
            move.landed(back_context.at[yy, xx, :, cc], sem_back.at[xx * 2 + cc, yy])
    for k in range(1, 8):
        t = lax.rem(spot + 8 - k, 8)
        move.landed(output.at[t], sem_out.at[t])
    move.finish(range(2, len(move.local)))


def backward_kernel(
    gu, gi, go, gs, query, key, value, context, back_context, joint_weight, first_far, tok_own, back_residual, vectors,
    out_o, out_i, out_u, out_s, out_joint, tokens_gradient, late,
    send_sem, local_sem, sem1, sem2, sem3, sem4, sem_y, sem_z, sem_g, sem_c, sem_x, sem_t, sem_s,
    r1u, r1i, r1o, r1s, r2u, r2i, r2o, r2s, r3u, r3i, r3o, r3s, r4u, r4i, r4o, r4s, ou, oi, oo, os_,
    joint, sums, turned, first_low, back_first, rc, rx, gj, ry, rz, sj, joint_land, gradient_low, small, small_all,
):
    bf16, f32 = jnp.bfloat16, jnp.float32
    y, x, z, c = place()
    spot = y * 4 + z
    mine = x * 2 + c
    me = number(y, x, z, c)
    other_core = at(y, x, z, 1 - c)
    across = at(y, 1 - x, z, c)
    down = at(1 - y, x, z, c)
    y1, x1 = jnp.where(c == 0, y, 1 - y), jnp.where(c == 0, 1 - x, x)
    y2, x2 = jnp.where(c == 0, 1 - y, y), jnp.where(c == 0, x, 1 - x)
    first, second = at(y1, x1, z, c), at(y2, x2, z, c)
    line = [lax.rem(z + k, 4) for k in range(1, 4)]
    line_devices = [at(y, x, zz, c) for zz in line]
    own, near1, near2 = y * 2 + x, y1 * 2 + x1, y2 * 2 + x2
    far = (1 - y) * 2 + 1 - x
    order = (far, near1, near2, own)
    group = quad(x, c)
    others = []
    for k in range(1, 32):
        t = lax.rem(me + k, 32)
        others.append((t, (t // 8, lax.rem(t, 8))))
    meet([device for _, device in others])
    move = Mover(send_sem, local_sem, other_core)
    zero = move.zero
    parts = (gu, gi, go, gs)
    halves = (ou, oi, oo, os_)
    results = (out_u, out_i, out_o, out_s)
    r1, r2 = (r1u, r1i, r1o, r1s), (r2u, r2i, r2o, r2s)
    r3, r4 = (r3u, r3i, r3o, r3s), (r4u, r4i, r4o, r4s)
    for i in (0, 2, 3, 1):
        for quarter in order:
            move.push(
                parts[i].at[quarter, :, 1 - c], r1[i].at[quarter], sem1.at[i, quarter], other_core
            )
    for i in range(4):
        move.keep(parts[i].at[:, :, c], halves[i])
    move.keep(first_far, first_low)

    def gather(i, quarter):
        move.landed(r1[i].at[quarter], sem1.at[zero + i, quarter])
        r1[i][quarter] = (wide(r1[i][quarter]) + wide(halves[i][quarter])).astype(r1[i].dtype)

    def stage2(i):
        for slot, quarter in ((1, far), (0, near1)):
            gather(i, quarter)
            move.push_made(
                lambda slot=slot, quarter=quarter: (
                    r1[i].at[quarter], r2[i].at[zero + slot], sem2.at[zero + i, zero + slot]
                ),
                first,
            )

    def stage3(i):
        gather(i, near2)
        move.landed(r2[i].at[zero + 1], sem2.at[zero + i, zero + 1])
        r1[i][near2] = (wide(r1[i][near2]) + wide(r2[i][1])).astype(r1[i].dtype)
        move.push_made(lambda: (r1[i].at[near2], r3[i], sem3.at[zero + i]), second)

    def stage4(i):
        gather(i, own)
        move.landed(r2[i].at[zero], sem2.at[zero + i, zero])
        move.landed(r3[i], sem3.at[zero + i])
        r1[i][own] = (wide(r1[i][own]) + wide(r2[i][0]) + wide(r3[i][...])).astype(r1[i].dtype)
        for k in range(3):
            move.push_made(
                lambda k=k: (r1[i].at[own, line[k]], r4[i].at[zero + k], sem4.at[zero + i, zero + k]),
                line_devices[k],
            )

    def stage5(i):
        total = wide(r1[i][own, z])
        for k in range(3):
            move.landed(r4[i].at[k], sem4.at[i, k])
            total = total + wide(r4[i][k])
        results[i][...] = total

    rows_all = query.shape[1]
    piece = tok_own.shape[1]
    rows = tok_own.shape[0] * piece
    width = tok_own.shape[2]
    scale = DH ** (-0.5)
    eye = jnp.eye(DH, 2 * DH, dtype=bf16)
    side_lane = lax.broadcasted_iota(jnp.int32, (BACK_ROWS, DH), 1)
    per_head = rows_all // BACK_ROWS
    between = {
        1: lambda: stage2(0),
        2: lambda: (stage2(2), stage2(3)),
        3: lambda: stage2(1),
        6: lambda: stage3(0),
        7: lambda: (stage3(2), stage3(3)),
        9: lambda: stage4(0),
        10: lambda: (stage4(2), stage4(3)),
        11: lambda: stage3(1),
    }
    for n in range(4):
        move.kept(n)
    for h in range(3):
        for k in range(rows_all // KEY_ROWS):
            turned[k] = dot(eye, key[h, k * KEY_ROWS : (k + 1) * KEY_ROWS, :], NT).astype(bf16)
        sums[...] = jnp.zeros_like(sums)
        lanes = slice(h * DH, (h + 1) * DH)

        def block(i, _):
            here = pl.ds(i * BACK_ROWS, BACK_ROWS)
            queries = query[h, here, :]
            backs = back_context[i // 2, lax.rem(i, 2)].reshape(BACK_ROWS, GROUP)[:, lanes]
            spread = jnp.sum(wide(backs) * wide(context[here, lanes]), axis=1, keepdims=True)
            high, mid, low = three(spread)
            side = jnp.where(
                side_lane == 0, -high, jnp.where(side_lane == 1, -mid, jnp.where(side_lane == 2, -low, 0.0))
            )
            widened = jnp.concatenate([backs, side.astype(bf16)], axis=1)

            def part(k, back_query):
                keys = pl.ds(k * KEY_ROWS, KEY_ROWS)
                chances = jnp.exp(dot(key[h, keys, :], queries, NT))
                back_scores = (chances * dot(value[h, keys, :], widened, NT)).astype(bf16)
                sums[keys, :DH] += dot(back_scores, queries[:, :DH])
                sums[keys, DH:] += dot(chances.astype(bf16), backs)
                return back_query + dot(turned[k], back_scores)

            back_query = jnp.zeros((DH, BACK_ROWS), f32)
            back_query = lax.fori_loop(0, rows_all // KEY_ROWS, part, back_query)
            joint[here, lanes] = (back_query * scale).T.astype(bf16)
            for step, action in between.items():
                if step // per_head == h:

                    @pl.when(i == step % per_head)
                    def _(action=action):
                        action()

            return 0

        lax.fori_loop(0, per_head, block, 0)
        joint[:, GROUP + h * DH : GROUP + (h + 1) * DH] = sums[:, :DH].astype(bf16)
        joint[:, 2 * GROUP + h * DH : 2 * GROUP + (h + 1) * DH] = sums[:, DH:].astype(bf16)

    for k in range(2):
        for yy in range(2):
            xx = lax.rem(x + 1 + k, 2)
            here = pl.ds((yy * 2 + xx) * rows, rows)
            back_first[yy, xx] = dot(joint[here, :], joint_weight[...], NT).astype(bf16).reshape(4, 2, piece, width)
            move.push(back_first.at[yy, xx, :, 1 - c], rc.at[yy, xx], sem_c.at[yy, xx], other_core)
    move.kept(4)
    grad = dot(first_low[...], joint[...], TN)
    lead = width // 32
    for block_at in range(32):
        gj[block_at // 16, block_at // 8 % 2, block_at % 8 // 2, block_at % 2] = grad[
            block_at * lead : (block_at + 1) * lead, :
        ].astype(bf16)
    move.push(gj.at[1 - y], ry, sem_y, down)
    for yy in range(2):
        move.landed(rc.at[yy, 1 - x], sem_c.at[yy, 1 - x])
        rc[yy, 1 - x] = (wide(rc[yy, 1 - x]) + wide(back_first[yy, 1 - x, :, c])).astype(bf16)
        move.push(rc.at[yy, 1 - x], rx.at[yy], sem_x.at[yy], across)
    stage4(1)
    shifts = jnp.sum(wide(joint[...]), axis=0, keepdims=True)
    small[...] = jnp.zeros_like(small)
    for k in range(8):
        for row, kind in ((2, 0), (3, 2)):
            start = kind * GROUP + k * lead
            small[mine * 8 + k, row : row + 1, :lead] = shifts[:, start : start + lead]
    move.landed(ry, sem_y)
    ry[...] = (wide(ry[...]) + wide(gj[y])).astype(bf16)
    for k in range(3):
        move.push(ry.at[:, line[k]], rz.at[k], sem_z.at[k], line_devices[k])
    for yy in range(2):
        move.landed(rc.at[yy, x], sem_c.at[yy, x])

    inputs = wide(tok_own[...].reshape(rows, width))
    centered = inputs - mean_of(inputs)
    inverse = lax.rsqrt(mean_of(centered * centered) + EPS)
    unit = centered * inverse
    halves_rows = []
    for yy in range(2):
        move.landed(rx.at[yy], sem_x.at[yy])
        whole = wide(rc[yy, x]) + wide(back_first[yy, x, :, c]) + wide(rx[yy])
        halves_rows.append(whole.reshape(rows // 2, width))
    back_one = jnp.concatenate(halves_rows, axis=0)
    scaled = back_one * vectors[0:1, :]
    back_tokens = back_residual[...] + inverse * (scaled - mean_of(scaled) - unit * mean_of(scaled * unit))
    gradient_low[...] = back_tokens.astype(bf16).reshape(8, piece, width)
    for k in range(1, 8):
        yy, zz = column(lax.rem(spot + k, 8))
        move.push(gradient_low.at[yy * 4 + zz], tokens_gradient.at[spot], sem_t.at[spot], at(yy, x, zz, c))
    kept = [move.keep(gradient_low.at[spot], tokens_gradient.at[spot])]
    gains = jnp.concatenate(
        [jnp.sum(back_one * unit, axis=0, keepdims=True), jnp.sum(back_one, axis=0, keepdims=True)], axis=0
    )
    for block_at in range(32):
        small[block_at, 0:2, :lead] = gains[:, block_at * lead : (block_at + 1) * lead]
    for t, device in others:
        move.push(small.at[t], small_all.at[me], sem_s.at[me], device)
    kept.append(move.keep(small.at[me], small_all.at[me]))

    total = wide(ry[:, z])
    for k in range(3):
        move.landed(rz.at[k], sem_z.at[k])
        total = total + wide(rz[k])
    sj[...] = total
    for xx, cc in group:
        move.push(sj.at[xx, cc], joint_land.at[mine], sem_g.at[mine], at(y, xx, z, cc))
    gone = move.keep(sj.at[x, c], joint_land.at[mine])
    for i in (0, 2, 3, 1):
        stage5(i)
    move.kept(gone)
    for xx, cc in group:
        move.landed(joint_land.at[xx * 2 + cc], sem_g.at[xx * 2 + cc])
    for g in range(4):
        for kind in range(3):
            start = kind * width + g * GROUP
            out_joint[:, start : start + GROUP] = joint_land[g, :, kind * GROUP : (kind + 1) * GROUP]
    for spot_kept in kept:
        move.kept(spot_kept)
    for t, _ in others:
        move.landed(small_all.at[t], sem_s.at[t])
    late[...] = jnp.sum(small_all[...], axis=0)
    for k in range(1, 8):
        t = lax.rem(spot + 8 - k, 8)
        move.landed(tokens_gradient.at[t], sem_t.at[t])
    move.finish()


def owner_device(
    tokens,
    lengths,
    first_gain,
    first_bias,
    joint_weight,
    query_bias,
    value_bias,
    output_weight,
    output_bias,
    second_gain,
    second_bias,
    inner_weight,
    inner_bias,
    outer_weight,
    outer_bias,
    cotangent,
):
    bf16, f32 = jnp.bfloat16, jnp.float32
    y, x, z, c = place()
    mine = x * 2 + c
    slots, piece, width = tokens.shape
    ff = inner_weight.shape[1]
    short = jnp.stack(
        [first_gain, first_bias, query_bias, value_bias, output_bias, second_gain, second_bias, outer_bias]
    )
    lead = short.shape[1]
    ff_piece = inner_bias.shape[0]
    small = jnp.concatenate(
        [
            jnp.pad(short, ((0, 0), (0, ff_piece - lead))),
            jnp.broadcast_to(inner_bias, (8, ff_piece)),
        ],
        axis=0,
    )
    hbm, vmem = pltpu.HBM, pltpu.VMEM
    dma, regular = pltpu.SemaphoreType.DMA, pltpu.SemaphoreType.REGULAR
    rows_all = 32 * piece
    natural = (2, 2, 4, 2, piece)
    length = lax.dynamic_slice(lengths, (y * 4 + z,), (1,))
    joint_four = jnp.transpose(joint_weight.reshape(lead, 3, 4, GROUP), (2, 0, 1, 3)).reshape(4, lead, 3 * GROUP)
    forward_outs = [
        ((rows_all, width), bf16, vmem),
        ((3, rows_all, 2 * DH), bf16, vmem),
        ((3, rows_all, 2 * DH), bf16, vmem),
        ((3, rows_all, 2 * DH), bf16, vmem),
        ((rows_all, GROUP), bf16, vmem),
        ((4, 2, 4, piece, GROUP), bf16, vmem),
        ((8, piece, width), bf16, hbm),
        ((8, piece, width), bf16, hbm),
        ((32,) + output_weight.shape, bf16, hbm),
        ((32,) + inner_weight.shape, bf16, hbm),
        ((32,) + outer_weight.shape, bf16, hbm),
        ((32,) + small.shape, bf16, vmem),
        ((width, 3 * GROUP), bf16, vmem),
    ]
    (
        first_low, query, key, value, context, context_rows, cot_own, tok_own, wo_all, wi_all, wu_all, small_all, joint_here
    ) = comm_call(
        forward_kernel,
        forward_outs,
        (length, tokens, cotangent, joint_four, output_weight, inner_weight, outer_weight, small),
        220, 16,
        [(32,), (8,), (3, 32), (32,), (4,), (4,), (4,), (8, 2), (4, 8), (8,)],
        [
            vmem((32, piece, width), bf16),
            vmem((2, 2, 4, 2, lead, 3 * GROUP), bf16),
            vmem((8, width), f32),
            vmem((3, 72, rows_all), bf16),
            vmem(natural + (GROUP,), bf16),
        ],
        0,
        [pltpu.SMEM, hbm, hbm, hbm, hbm, hbm, hbm, hbm],
    )
    vectors = jnp.transpose(small_all[:, :2, :lead], (1, 0, 2)).reshape(2, width).astype(f32)
    rows = 8 * piece
    grid = (4, 4, 2)
    kinds = [
        (outer_weight.shape, bf16),
        (inner_weight.shape, bf16),
        (output_weight.shape, bf16),
        ((8, 128), f32),
    ]
    gu, gi, go, gs, output, back_context, back_residual = comm_call(
        feed_kernel,
        [(grid + shape, dtype, hbm) for shape, dtype in kinds]
        + [
            (tokens.shape, bf16, hbm),
            (natural + (GROUP,), bf16, vmem),
            ((rows, width), f32, vmem),
        ],
        (
            length, context_rows.reshape(4, 8, piece, GROUP), tok_own, cot_own, wo_all.reshape(width, width), small_all,
            wi_all.reshape(width, ff), wu_all.reshape(grid + outer_weight.shape),
        ),
        20, 20, [(8,), (4, 2)],
        [vmem(grid + shape, dtype) for shape, dtype in kinds]
        + [
            vmem((width, ff), bf16),
            vmem((4, 8, piece, GROUP), bf16),
            vmem((8, width), f32),
            vmem((1, ff), f32),
            vmem((rows, ff), bf16),
            vmem((rows, ff), bf16),
            vmem((8, piece, width), bf16),
        ],
        1,
        [pltpu.SMEM] + [vmem] * 5 + [hbm] * 2,
    )
    out_o, out_i, out_u, out_s, joint_shard, tokens_gradient, late = comm_call(
        backward_kernel,
        [
            (output_weight.shape, f32, vmem),
            (inner_weight.shape, f32, vmem),
            (outer_weight.shape, f32, vmem),
            ((8, 128), f32, vmem),
            (joint_weight.shape, f32, vmem),
            (tokens.shape, bf16, hbm),
            ((8, 128), f32, vmem),
        ],
        (
            gu, gi, go, gs, query, key, value, context, back_context, joint_here, first_low, tok_own, back_residual, vectors,
        ),
        110, 16,
        [(4, 4), (4, 2), (4,), (4, 3), (), (3,), (4,), (2, 2), (2,), (8,), (32,)],
        [vmem((4, 4) + shape, dtype) for shape, dtype in kinds]
        + [vmem((2, 4) + shape, dtype) for shape, dtype in kinds]
        + [vmem((4,) + shape, dtype) for shape, dtype in kinds]
        + [vmem((3,) + shape, dtype) for shape, dtype in kinds]
        + [vmem((4, 4) + shape, dtype) for shape, dtype in kinds]
        + [
            vmem((rows_all, 3 * GROUP), bf16),
            vmem((rows_all, 2 * DH), f32),
            vmem((rows_all // KEY_ROWS, DH, KEY_ROWS), bf16),
            vmem((rows_all, width), bf16),
            vmem(natural + (width,), bf16),
            vmem((2, 2, 4, piece, width), bf16),
            vmem((2, 4, piece, width), bf16),
            vmem((2, 2, 4, 2, lead, 3 * GROUP), bf16),
            vmem((2, 4, 2, lead, 3 * GROUP), bf16),
            vmem((3, 2, 2, lead, 3 * GROUP), bf16),
            vmem((2, 2, lead, 3 * GROUP), f32),
            vmem((4, lead, 3 * GROUP), f32),
            vmem((8, piece, width), bf16),
            vmem((32, 8, 128), f32),
            vmem((32, 8, 128), f32),
        ],
        2,
        [hbm] * 4 + [vmem] * 6 + [hbm] + [vmem] * 3,
    )
    count = jnp.sum(lengths).astype(f32) * width
    stats = jnp.sqrt(out_s[5, :3] / count + 1e-06)
    return (
        output,
        tokens_gradient,
        late[0, :lead],
        late[1, :lead],
        joint_shard,
        late[2, :lead],
        late[3, :lead],
        out_o,
        out_s[3, :lead],
        out_s[1, :lead],
        out_s[2, :lead],
        out_i,
        out_s[4, : inner_bias.shape[0]],
        out_u,
        out_s[0, :lead],
        stats,
    )


def solution(mesh):
    in_specs = (
        P(None, ("head", "blk"), None),
        P(),
        P(("head", "blk")),
        P(("head", "blk")),
        P(("head", "blk"), None),
        P(("head", "blk")),
        P(("head", "blk")),
        P(("head", "blk"), None),
        P(("head", "blk")),
        P(("head", "blk")),
        P(("head", "blk")),
        P(("head", "blk"), None),
        P(("head", "blk")),
        P(("head", "blk"), None),
        P(("head", "blk")),
        P(None, ("head", "blk"), None),
    )
    out_specs = (
        P(None, ("head", "blk"), None),
        P(None, ("head", "blk"), None),
        P(("head", "blk")),
        P(("head", "blk")),
        P(("head", "blk"), None),
        P(("head", "blk")),
        P(("head", "blk")),
        P(("head", "blk"), None),
        P(("head", "blk")),
        P(("head", "blk")),
        P(("head", "blk")),
        P(("head", "blk"), None),
        P(("head", "blk")),
        P(("head", "blk"), None),
        P(("head", "blk")),
        P(),
    )
    small_slice = dict(mesh.shape) == {"head": 4, "blk": 8}
    device_work = owner_device if small_slice else on_device
    return jax.shard_map(
        device_work, mesh=mesh, in_specs=in_specs, out_specs=out_specs, check_vma=False
    )
```

profile of v0, /device:TPU:0, one launch (start us, length us, event | category | flops | bytes accessed | tf_op | source)
XLA Modules:
  0.0 322.3 jit_solution(13888391820385840383)
XLA Ops:
  0.7 1.2 dynamic_slice.3.length
  1.9 1.1 reshape.58
  3.0 0.1 copy.37
  3.1 0.8 reshape.59.wj
  3.9 0.7 broadcast_in_dim.3
  4.5 0.8 stack.35
  5.3 0.6 fusion.1.small
  5.9 130.3 %shard_map.279 = (bf16[2048,768]{1,0:T(8,128)(2,1)}, bf16[3,2048,128]{2,1,0:T(8,128)(2,1)}, bf16[3,2048,128]{2,1,0:T(8,128)(2,1)}, bf16[3,2048,128]{2,1,0:T(8,12...) custom-call(s32[1]{0:T(128)} %dynamic_slice.3.length, ...), custom_call_target="tpu_custom_call" | custom-call | tf_op jit(solution)/shard_map/pallas_call | solution.py:719
  136.2 48.7 %shard_map.280 = (bf16[4,4,2,96,768]{4,3,2,1,0:T(8,128)(2,1)}, bf16[4,4,2,24,3072]{4,3,2,1,0:T(8,128)(2,1)}, bf16[4,4,2,24,768]{4,3,2,1,0:T(8,128)(2,1)}, f32[4,...) custom-call(s32[1]{0:T(128)} %dynamic_slice.3.length, ...), custom_call_target="tpu_custom_call" | custom-call | tf_op jit(solution)/shard_map/pallas_call | solution.py:719
  185.0 0.9 convert_bitcast_fusion
  185.8 0.7 reshape.64.vectors
  186.5 0.0 copy-start.6
  186.5 0.0 copy-start
  186.5 126.0 %shard_map.281 = (f32[24,768]{1,0:T(8,128)}, f32[24,3072]{1,0:T(8,128)}, f32[96,768]{1,0:T(8,128)}, f32[8,128]{1,0:T(8,128)}, f32[24,2304]{1,0:T(8,128)}, /*index=5*/bf16[8,64,768]{2,1,0:T(8,128)(2,1)}, f32[8,128]{1,0:T(8,128)}) custom-call(bf16[4,4,2,96,768]{4,3,2,1,0:T(8,128)(2,1)} %get-tuple-element.51.gu, ...), custom_call_target="tpu_custom_call" | custom-call | tf_op jit(solution)/shard_map/pallas_call | solution.py:719
  312.5 0.0 copy-start.1
  312.5 1.4 slice_bitcast_fusion
  313.9 0.0 copy-done.6
  313.9 0.6 reduce_sum.9
  315.2 1.2 sqrt_bitcast_fusion
  316.4 1.2 slice_bitcast_fusion.1
  317.6 0.0 copy-done
  317.6 0.0 copy-start.4
  317.6 0.0 copy-start.5
  317.6 0.0 copy-start.3
  317.6 0.9 copy.44
  318.5 0.0 copy-done.1
  318.5 0.0 copy-start.2
  318.5 0.9 copy.45
  319.4 0.0 copy-done.4
  319.4 0.7 copy.46
  320.1 0.0 copy-done.5
  320.1 0.6 copy.47
  320.7 0.0 copy-done.3
  320.7 0.7 copy.48
  321.4 0.0 copy-done.2
  321.4 0.7 copy.49
  (1 shorter events, 0.0 us)
Async XLA Ops:
  186.5 127.4 %copy-start.6 = (s32[8]{0:T(128)S(1)}, s32[8]{0:T(128)}, u32[]{:S(2)}) copy-start(s32[8]{0:T(128)} %param.17) | copy-start | bytes 100
  186.5 131.1 %copy-start = (bf16[8,64,768]{2,1,0:T(8,128)(2,1)S(1)}, bf16[8,64,768]{2,1,0:T(8,128)(2,1)}, u32[]{:S(2)}) copy-start(bf16[8,64,768]{2,1,0:T(8,128)(2,1)} %get-tuple-element.98) | copy-start | bytes 2359300
  312.5 6.0 %copy-start.1 = (bf16[8,64,768]{2,1,0:T(8,128)(2,1)S(1)}, bf16[8,64,768]{2,1,0:T(8,128)(2,1)}, u32[]{:S(2)}) copy-start(bf16[8,64,768]{2,1,0:T(8,128)(2,1)} %get-tuple-element.99) | copy-start | bytes 2359300
  317.6 1.8 copy-start.4
  317.6 2.5 copy-start.5
  317.6 3.1 copy-start.3
  318.5 2.9 copy-start.2
where the time goes:
time: 328 us; the launch traced here: 322 us
  Pallas kernels  305 us (93%)
  local copies, waits for them, and re-layouts  12.4 us (4%)
    pallas_call x3, Pallas kernels, comm_call(): pl.pallas_call(kernel, out_shape=[jax.ShapeDtypeStruct(shape, dtype) for...  305 us

commit v1 on v0

--- a/solution.py
+++ b/solution.py
@@ -412,10 +412,10 @@
     def push(self, source, target, sem, device):
         self.push_made(lambda: (source, target, sem), device)
 
-    def push_made(self, make, device):
+    def push_made(self, make, device, when=None):
         spot = len(self.sent)
-        self.sent.append((make, spot, device))
-        self.copy(make, spot, device).start()
+        self.sent.append((make, spot, device, when))
+        under(when, lambda: self.copy(make, spot, device).start())
 
     def copy(self, make, spot, device):
         source, target, sem = make()
@@ -434,10 +434,20 @@
         remote(target, target, self.send_sem.at[self.zero], sem, self.anyone).wait_recv()
 
     def finish(self, kept=()):
-        for parts in self.sent:
-            self.copy(*parts).wait_send()
+        for make, spot, device, when in self.sent:
+            under(when, lambda: self.copy(make, spot, device).wait_send())
         for spot in kept:
             self.kept(spot)
+
+
+def under(when, action):
+    if when is None:
+        action()
+    else:
+
+        @pl.when(when)
+        def _():
+            action()
 
 
 def remote(source, target, send_sem, recv_sem, device):
@@ -459,9 +469,9 @@
 
 def forward_kernel(
     length, tokens, cotangent, wj, wo, wi, wu, small,
-    first_low, query, key, value, context, context_rows, cot_own, tok_own, wo_all, wi_all, wu_all, small_all, wj_flat,
+    first_far, query_far, key_far, value_far, context, context_rows, cot_own, tok_own, wo_all, wi_all, wu_all, small_all, wj_flat,
     send_sem, local_sem, tok_sem, cot_sem, weight_sem, small_sem, wja_sem, wjb_sem, wjc_sem, ctx_send, ctx_recv,
-    ctx_local, tok_all, wj_all, vectors, turned, mixed_low,
+    ctx_local, tok_all, wj_all, vectors, turned, mixed_low, score_a, score_b, straight_low, first_low, query, key, value,
 ):
     y, x, z, c = place()
     mine = number(y, x, z, c)
@@ -476,11 +486,20 @@
     first, second = at(y1, x1, z, c), at(y2, x2, z, c)
     spots = [column(lax.rem(spot + k, 8)) for k in range(1, 8)]
     back_spots = [column(lax.rem(spot + 8 - k, 8)) for k in range(1, 8)]
-    lines = [lax.rem(z + 4 - k, 4) for k in range(4)]
     ahead = [at(y, x, lax.rem(z + k, 4), c) for k in range(1, 4)]
+    inside = jnp.logical_or(z == 1, z == 2)
+    lines = [
+        z,
+        jnp.where(z == 0, 1, z - 1),
+        jnp.where(z == 0, 2, jnp.where(z == 3, 1, z + 1)),
+        jnp.where(z < 2, 3, 0),
+    ]
+    onward = [z + 1, z - 1, jnp.where(z == 1, 0, 3)]
+    away, back = at(y, x, jnp.where(z < 3, z + 1, z - 1), c), at(y, x, jnp.maximum(z - 1, 0), c)
+    onward = [at(y, x, lax.rem(zz + 4, 4), c) for zz in onward]
     line_blocks = [number(y, x, zz, c) for zz in lines]
     first_blocks = [number(y1, x1, zz, c) for zz in lines]
-    second_blocks = [number(yy, xx, zz, c) for yy, xx in ((y2, x2), (1 - y, 1 - x)) for zz in lines]
+    second_blocks = [number(yy, xx, zz, c) for zz in lines for yy, xx in ((y2, x2), (1 - y, 1 - x))]
     core_blocks = [number(yy, xx, zz, 1 - c) for yy in range(2) for xx in range(2) for zz in range(4)]
     group = quad(x, c)
     meet([at(yy, x, zz, c) for yy, zz in spots] + [across, other_core, diagonal])
@@ -488,19 +507,7 @@
     sources = (wo, wi, wu)
     wholes = (wo_all, wi_all, wu_all)
 
-    for yy, zz in spots:
-        move.push(tokens.at[yy * 4 + zz], tok_all.at[mine], tok_sem.at[mine], at(yy, x, zz, c))
-    for xx, cc in group:
-        move.push(wj.at[xx * 2 + cc], wj_all.at[y, x, z, c], wja_sem.at[quarter], at(y, xx, z, cc))
-    move.keep(wj.at[quarter], wj_all.at[y, x, z, c])
-    move.push(tokens.at[spot], tok_all.at[mine], tok_sem.at[mine], across)
-    move.push(tokens.at[spot], tok_all.at[mine], tok_sem.at[mine], other_core)
-    move.keep(tokens.at[spot], tok_all.at[mine])
-    for device in ahead + [first, second, other_core]:
-        move.push(small, small_all.at[mine], small_sem.at[mine], device)
-    move.keep(small, small_all.at[mine])
-
-    def hand(block, own, device):
+    def hand(block, own, device, when=None):
         for i in range(3):
             move.push_made(
                 lambda i=i: (
@@ -509,6 +516,7 @@
                     weight_sem.at[move.zero + i, block],
                 ),
                 device,
+                when,
             )
 
     def arrive(block):
@@ -521,47 +529,77 @@
             for device in devices:
                 move.push(small_all.at[block], small_all.at[block], small_sem.at[block], device)
 
-    for device in ahead:
-        hand(mine, True, device)
+    def spread(block, own):
+        for device in (first, second, other_core):
+            hand(block, own, device)
+
+    def line_arrived(k):
+        arrive(line_blocks[k])
+        hand(line_blocks[k], False, onward[k - 1], inside)
+        spread(line_blocks[k], False)
+
+    def second_hand(k):
+        arrive(first_blocks[k])
+        hand(first_blocks[k], False, second)
+        hand(first_blocks[k], False, other_core)
+
+    def last_hand(k):
+        for b in second_blocks[2 * k : 2 * k + 2]:
+            arrive(b)
+            hand(b, False, other_core)
+
+    for device in ahead + [first, second, other_core]:
+        move.push(small, small_all.at[mine], small_sem.at[mine], device)
+    for xx, cc in group:
+        move.push(wj.at[xx * 2 + cc], wj_all.at[y, x, z, c], wja_sem.at[quarter], at(y, xx, z, cc))
+    move.keep(wj.at[quarter], wj_all.at[y, x, z, c])
+    move.keep(tokens.at[spot], tok_all.at[mine])
+    move.keep(small, small_all.at[mine])
+    for yy, zz in spots:
+        move.push(tokens.at[yy * 4 + zz], tok_all.at[mine], tok_sem.at[mine], at(yy, x, zz, c))
+    for device in (across, other_core):
+        move.push(tokens.at[spot], tok_all.at[mine], tok_sem.at[mine], device)
+    spread(mine, True)
     for source, whole in zip(sources, wholes):
         move.keep(source, whole.at[mine])
-    hand(mine, True, first)
-    hand(mine, True, second)
-    hand(mine, True, other_core)
+
+    def slice_onward(zz, device, when):
+        move.push_made(lambda: (wj_all.at[y, :, zz], wj_all.at[y, :, zz], wjb_sem.at[zz]), device, when)
 
     for xx, cc in group:
         move.landed(wj_all.at[y, xx, z, cc], wja_sem.at[xx * 2 + cc])
     move.kept(0)
-    for device in ahead:
-        move.push(wj_all.at[y, :, z], wj_all.at[y, :, z], wjb_sem.at[z], device)
+    slice_onward(z, away, None)
+    slice_onward(z, back, inside)
     move.push(wj_all.at[y, :, z], wj_all.at[y, :, z], wjc_sem.at[z], down)
     pass_small(line_blocks[1:], (first, second, other_core))
+    pass_small(first_blocks, (second, other_core))
+    for k in range(1, 4):
+        zz = lines[k]
+        move.landed(wj_all.at[y, :, zz], wjb_sem.at[zz])
+        slice_onward(zz, onward[k - 1], inside)
+        move.push(wj_all.at[y, :, zz], wj_all.at[y, :, zz], wjc_sem.at[zz], down)
+    pass_small(second_blocks, (other_core,))
     for yy, zz in back_spots:
         block = number(yy, x, zz, c)
         move.landed(tok_all.at[block], tok_sem.at[block])
         move.push(tok_all.at[block], tok_all.at[block], tok_sem.at[block], across)
         move.push(tok_all.at[block], tok_all.at[block], tok_sem.at[block], other_core)
-    for zz in lines[1:]:
-        move.landed(wj_all.at[y, :, zz], wjb_sem.at[zz])
-        move.push(wj_all.at[y, :, zz], wj_all.at[y, :, zz], wjc_sem.at[zz], down)
-    for yy, zz in spots:
-        move.push(cotangent.at[yy * 4 + zz], cot_own.at[spot], cot_sem.at[spot], at(yy, x, zz, c))
-    move.keep(cotangent.at[spot], cot_own.at[spot])
-    pass_small(first_blocks, (second, other_core))
-    pass_small(second_blocks, (other_core,))
+    hand(mine, True, away)
+    hand(mine, True, back, inside)
+    second_hand(0)
     for yy, zz in [(y, z)] + back_spots:
         block = number(yy, 1 - x, zz, c)
         move.landed(tok_all.at[block], tok_sem.at[block])
         move.push(tok_all.at[block], tok_all.at[block], tok_sem.at[block], other_core)
-    for block in line_blocks[1:]:
-        arrive(block)
-        hand(block, False, first)
-        hand(block, False, second)
-        hand(block, False, other_core)
     for block in core_blocks:
         move.landed(small_all.at[block], small_sem.at[block])
     for zz in lines:
         move.landed(wj_all.at[1 - y, :, zz], wjc_sem.at[zz])
+    line_arrived(1)
+    for yy, zz in spots:
+        move.push(cotangent.at[yy * 4 + zz], cot_own.at[spot], cot_sem.at[spot], at(yy, x, zz, c))
+    move.keep(cotangent.at[spot], cot_own.at[spot])
     for yy, zz in [(y, z)] + back_spots:
         for xx in (x, 1 - x):
             block = number(yy, xx, zz, 1 - c)
@@ -611,72 +649,97 @@
             value[h, here, :] = jnp.concatenate([low_v[:, here_h], three_lanes], axis=1)
         return 0
 
-    lax.fori_loop(0, rows // ROWS, project, 0)
+    for i in range(rows // ROWS):
+        project(i, 0)
+    for source, target in ((first_low, first_far), (key, key_far), (value, value_far)):
+        move.keep(source, target)
     eye = jnp.eye(72, 2 * DH, dtype=jnp.bfloat16)
     for h in range(3):
         turned[h] = dot(eye, value[h], NT).astype(jnp.bfloat16)
-    side = lax.broadcasted_iota(jnp.int32, (DH, ROWS), 0)
-
-    def ctx_piece(j, cc):
-        yy, xx, zz = j // 4, lax.rem(j // 2, 2), pl.ds(lax.rem(j, 2) * 2, 2)
-        return mixed_low.at[yy, xx, zz, cc], context_rows.at[quarter, yy, zz]
-
-    def block(j, _):
-        here = pl.ds(j * ROWS, ROWS)
-        whole = []
-        for h in range(3):
-            scores = dot(key[h], query[h, here, :], NT)
-            best = jnp.max(scores, axis=0, keepdims=True)
-            weights = jnp.exp(scores - best).astype(jnp.bfloat16)
-            mixed = dot(turned[h], weights)
-            total = mixed[DH : DH + 1, :]
-            mixed = mixed[:DH, :] / total
-            log_total = best + jnp.log(total)
-            high = log_total.astype(jnp.bfloat16).astype(jnp.float32)
-            middle = (log_total - high).astype(jnp.bfloat16).astype(jnp.float32)
-            low = log_total - high - middle
-            extra = jnp.where(
-                side == 0, 1.0, jnp.where(side == 1, -high, jnp.where(side == 2, -middle, jnp.where(side == 3, -low, 0.0)))
-            )
-            straight = jnp.concatenate([mixed, extra], axis=0).T
-            query[h, here, DH:] = straight[:, DH:].astype(jnp.bfloat16)
-            whole.append(straight[:, :DH])
-        mixed = jnp.concatenate(whole, axis=1)
-        yy, xx, zz = j // 4, lax.rem(j // 2, 2), lax.rem(j, 2) * 2
-        low = mixed.astype(jnp.bfloat16)
-        context[here, :] = low
-        piece = tokens.shape[1]
-        for k in range(2):
+    wider = score_a.shape[1]
+    side = lax.broadcasted_iota(jnp.int32, (DH, wider), 0)
+    chunk = 512
+    units = 3 * rows // wider
+
+    def ctx_copy(j, cc, for_local, for_remote):
+        yy, xx = j // 2, lax.rem(j, 2)
+        source, target = mixed_low.at[yy, xx, :, cc], context_rows.at[quarter, yy]
+        here = jnp.logical_and(xx == x, c == cc)
+
+        @pl.when(here)
+        def _():
+            for_local(pltpu.make_async_copy(source, target, ctx_local.at[j]))
+
+        @pl.when(jnp.logical_not(here))
+        def _():
+            for_remote(remote(source, target, ctx_send.at[j, cc], ctx_recv.at[quarter, j], at(y, xx, z, cc)))
+
+    def score_chunk(held, h, queries, k, best):
+        fresh = dot(key[h, k * chunk : (k + 1) * chunk, :], queries, NT)
+        held[k * chunk : (k + 1) * chunk, :] = fresh
+        return jnp.maximum(best, jnp.max(fresh, axis=0, keepdims=True))
+
+    lowest = jnp.full((1, wider), -jnp.inf, jnp.float32)
+    start = lowest
+    for k in range(rows // chunk):
+        start = score_chunk(score_a, 0, query[0, :wider, :], k, start)
+
+    def unit(u, best, held, fresh):
+        j = u // 3
+        h = u - 3 * j
+        u_next = jnp.minimum(u + 1, units - 1)
+        j_next = u_next // 3
+        h_next = u_next - 3 * j_next
+        here = pl.ds(j * wider, wider)
+        queries = query[h_next, pl.ds(j_next * wider, wider), :]
+        best_next = lowest
+        mixed = jnp.zeros((72, wider), jnp.float32)
+        for k in range(rows // chunk):
+            keys = slice(k * chunk, (k + 1) * chunk)
+            weights = jnp.exp(held[keys, :] - best).astype(jnp.bfloat16)
+            mixed = mixed + dot(turned[h, :, keys], weights)
+            best_next = score_chunk(fresh, h_next, queries, k, best_next)
+        total = mixed[DH : DH + 1, :]
+        mixed = mixed[:DH, :] / total
+        high, mid, low = three(best + jnp.log(total))
+        extra = jnp.where(
+            side == 0, 1.0, jnp.where(side == 1, -high, jnp.where(side == 2, -mid, jnp.where(side == 3, -low, 0.0)))
+        )
+        straight = jnp.concatenate([mixed, extra], axis=0).T
+        query[h, here, DH:] = straight[:, DH:].astype(jnp.bfloat16)
+        straight_low[h] = straight[:, :DH].astype(jnp.bfloat16)
+
+        @pl.when(h == 2)
+        def _():
+            whole = jnp.concatenate([straight_low[k] for k in range(3)], axis=1)
+            context[here, :] = whole
+            mixed_low[j // 2, lax.rem(j, 2)] = whole.reshape(4, 2, tokens.shape[1], GROUP)
             for cc in range(2):
-                start = (k * 2 + cc) * piece
-                mixed_low[yy, xx, zz + k, cc] = low[start : start + piece]
-        for cc in range(2):
-            source, target = ctx_piece(j, cc)
-
-            @pl.when(jnp.logical_and(xx == x, c == cc))
-            def _():
-                pltpu.make_async_copy(source, target, ctx_local.at[j]).start()
-
-            @pl.when(jnp.logical_not(jnp.logical_and(xx == x, c == cc)))
-            def _():
-                remote(source, target, ctx_send.at[j, cc], ctx_recv.at[quarter, j], at(y, xx, z, cc)).start()
-
-        @pl.when(j == 2)
-        def _():
-            for b in first_blocks:
-                arrive(b)
-                hand(b, False, second)
-                hand(b, False, other_core)
-
-        @pl.when(j == 6)
-        def _():
-            for b in second_blocks:
-                arrive(b)
-                hand(b, False, other_core)
-
-        return 0
-
-    lax.fori_loop(0, rows // ROWS, block, 0)
+                ctx_copy(j, cc, lambda copy: copy.start(), lambda copy: copy.start())
+
+        return best_next
+
+    def pair(p, best):
+        best = unit(2 * p, best, score_a, score_b)
+        best = unit(2 * p + 1, best, score_b, score_a)
+        for when, action in (
+            (0, lambda: second_hand(1)),
+            (1, lambda: line_arrived(2)),
+            (2, lambda: (second_hand(2), last_hand(0))),
+            (3, lambda: line_arrived(3)),
+            (4, lambda: (second_hand(3), last_hand(1))),
+        ):
+
+            @pl.when(p == when)
+            def _(action=action):
+                action()
+
+        return best
+
+    lax.fori_loop(0, units // 2, pair, start)
+    move.keep(query, query_far)
+    last_hand(2)
+    last_hand(3)
     for yy, zz in back_spots:
         move.landed(cot_own.at[yy * 4 + zz], cot_sem.at[yy * 4 + zz])
     for b in core_blocks:
@@ -688,27 +751,14 @@
         tok_copies[-1].start()
 
     def settle(j, _):
-        xx = lax.rem(j // 2, 2)
         for cc in range(2):
-            source, target = ctx_piece(j, cc)
-
-            @pl.when(jnp.logical_and(xx == x, c == cc))
-            def _():
-                pltpu.make_async_copy(source, target, ctx_local.at[j]).wait()
-
-            @pl.when(jnp.logical_not(jnp.logical_and(xx == x, c == cc)))
-            def _():
-                remote(source, target, ctx_send.at[j, cc], ctx_recv.at[quarter, j], at(y, xx, z, cc)).wait_send()
-
+            ctx_copy(j, cc, lambda copy: copy.wait(), lambda copy: copy.wait_send())
         return 0
 
-    lax.fori_loop(0, rows // ROWS, settle, 0)
+    lax.fori_loop(0, 4, settle, 0)
     for xx, cc in group:
         for yy in range(2):
-            for half in range(2):
-                j = yy * 4 + x * 2 + half
-                target = context_rows.at[xx * 2 + cc, yy, pl.ds(half * 2, 2)]
-                move.landed(target, ctx_recv.at[xx * 2 + cc, j])
+            move.landed(context_rows.at[xx * 2 + cc, yy], ctx_recv.at[xx * 2 + cc, yy * 2 + x])
     move.finish(range(3, len(move.local)))
     for copy in tok_copies:
         copy.wait()
@@ -1197,10 +1247,10 @@
     length = lax.dynamic_slice(lengths, (y * 4 + z,), (1,))
     joint_four = jnp.transpose(joint_weight.reshape(lead, 3, 4, GROUP), (2, 0, 1, 3)).reshape(4, lead, 3 * GROUP)
     forward_outs = [
-        ((rows_all, width), bf16, vmem),
-        ((3, rows_all, 2 * DH), bf16, vmem),
-        ((3, rows_all, 2 * DH), bf16, vmem),
-        ((3, rows_all, 2 * DH), bf16, vmem),
+        ((rows_all, width), bf16, hbm),
+        ((3, rows_all, 2 * DH), bf16, hbm),
+        ((3, rows_all, 2 * DH), bf16, hbm),
+        ((3, rows_all, 2 * DH), bf16, hbm),
         ((rows_all, GROUP), bf16, vmem),
         ((4, 2, 4, piece, GROUP), bf16, vmem),
         ((8, piece, width), bf16, hbm),
@@ -1217,14 +1267,21 @@
         forward_kernel,
         forward_outs,
         (length, tokens, cotangent, joint_four, output_weight, inner_weight, outer_weight, small),
-        220, 16,
-        [(32,), (8,), (3, 32), (32,), (4,), (4,), (4,), (8, 2), (4, 8), (8,)],
+        220, 24,
+        [(32,), (8,), (3, 32), (32,), (4,), (4,), (4,), (4, 2), (4, 4), (4,)],
         [
             vmem((32, piece, width), bf16),
             vmem((2, 2, 4, 2, lead, 3 * GROUP), bf16),
             vmem((8, width), f32),
             vmem((3, 72, rows_all), bf16),
             vmem(natural + (GROUP,), bf16),
+            vmem((rows_all, 512), f32),
+            vmem((rows_all, 512), f32),
+            vmem((3, 512, DH), bf16),
+            vmem((rows_all, width), bf16),
+            vmem((3, rows_all, 2 * DH), bf16),
+            vmem((3, rows_all, 2 * DH), bf16),
+            vmem((3, rows_all, 2 * DH), bf16),
         ],
         0,
         [pltpu.SMEM, hbm, hbm, hbm, hbm, hbm, hbm, hbm],

time: 328 us -> 295 us (0.90)
  Pallas kernels: 305 us -> 272 us
    pallas_call x3, Pallas kernels: 305 us -> 272 us  [comm_call(): pl.pallas_call(kernel, out_shape=[jax.ShapeDtypeStruct(shape, dtype) for...]
where the time goes in v1:
time: 295 us; the launch traced here: 290 us
  Pallas kernels  272 us (92%)
  local copies, waits for them, and re-layouts  12.4 us (4%)
  other arithmetic  3.28 us (1%)
    pallas_call x3, Pallas kernels, comm_call(): pl.pallas_call(kernel, out_shape=[jax.ShapeDtypeStruct(shape, dtype) for...  272 us

profile of v1, /device:TPU:0, one launch (start us, length us, event | category | flops | bytes accessed | tf_op | source)
XLA Modules:
  0.0 289.7 jit_solution(2937093450668808946)
XLA Ops:
  0.7 1.2 dynamic_slice.3.length
  1.9 1.1 reshape.58
  3.0 0.1 copy.37
  3.1 0.8 reshape.59.wj
  3.9 0.7 broadcast_in_dim.3
  4.5 0.8 stack.35
  5.3 0.6 fusion.1.small
  5.9 110.5 %shard_map.279 = (bf16[2048,768]{1,0:T(8,128)(2,1)}, bf16[3,2048,128]{2,1,0:T(8,128)(2,1)}, bf16[3,2048,128]{2,1,0:T(8,128)(2,1)}, bf16[3,2048,128]{2,1,0:T(8,12...) custom-call(s32[1]{0:T(128)} %dynamic_slice.3.length, ...), custom_call_target="tpu_custom_call" | custom-call | tf_op jit(solution)/shard_map/pallas_call | solution.py:769
  116.5 44.5 %shard_map.280 = (bf16[4,4,2,96,768]{4,3,2,1,0:T(8,128)(2,1)}, bf16[4,4,2,24,3072]{4,3,2,1,0:T(8,128)(2,1)}, bf16[4,4,2,24,768]{4,3,2,1,0:T(8,128)(2,1)}, f32[4,...) custom-call(s32[1]{0:T(128)} %dynamic_slice.3.length, ...), custom_call_target="tpu_custom_call" | custom-call | tf_op jit(solution)/shard_map/pallas_call | solution.py:769
  161.0 0.9 convert_bitcast_fusion
  161.9 0.7 reshape.64.vectors
  162.6 0.0 copy-start.6
  162.6 0.0 copy-start
  162.6 117.0 %shard_map.281 = (f32[24,768]{1,0:T(8,128)}, f32[24,3072]{1,0:T(8,128)}, f32[96,768]{1,0:T(8,128)}, f32[8,128]{1,0:T(8,128)}, f32[24,2304]{1,0:T(8,128)}, /*index=5*/bf16[8,64,768]{2,1,0:T(8,128)(2,1)}, f32[8,128]{1,0:T(8,128)}) custom-call(bf16[4,4,2,96,768]{4,3,2,1,0:T(8,128)(2,1)} %get-tuple-element.51.gu, ...), custom_call_target="tpu_custom_call" | custom-call | tf_op jit(solution)/shard_map/pallas_call | solution.py:769
  279.6 0.0 copy-start.1
  279.6 1.4 slice_bitcast_fusion
  281.0 0.0 copy-done.6
  281.0 0.6 reduce_sum.9
  282.3 1.2 sqrt_bitcast_fusion
  283.5 1.2 slice_bitcast_fusion.1
  284.7 0.0 copy-done
  284.7 0.0 copy-start.4
  284.7 0.0 copy-start.5
  284.7 0.0 copy-start.3
  284.7 0.9 copy.44
  285.6 0.0 copy-done.1
  285.6 0.0 copy-start.2
  285.6 0.9 copy.45
  286.5 0.0 copy-done.4
  286.5 0.7 copy.46
  287.2 0.0 copy-done.5
  287.2 0.6 copy.47
  287.8 0.0 copy-done.3
  287.8 0.7 copy.48
  288.5 0.0 copy-done.2
  288.5 0.7 copy.49
  (1 shorter events, 0.0 us)
Async XLA Ops:
  162.6 118.4 %copy-start.6 = (s32[8]{0:T(128)S(1)}, s32[8]{0:T(128)}, u32[]{:S(2)}) copy-start(s32[8]{0:T(128)} %param.17) | copy-start | bytes 100
  162.6 122.1 %copy-start = (bf16[8,64,768]{2,1,0:T(8,128)(2,1)S(1)}, bf16[8,64,768]{2,1,0:T(8,128)(2,1)}, u32[]{:S(2)}) copy-start(bf16[8,64,768]{2,1,0:T(8,128)(2,1)} %get-tuple-element.98) | copy-start | bytes 2359300
  279.6 6.0 %copy-start.1 = (bf16[8,64,768]{2,1,0:T(8,128)(2,1)S(1)}, bf16[8,64,768]{2,1,0:T(8,128)(2,1)}, u32[]{:S(2)}) copy-start(bf16[8,64,768]{2,1,0:T(8,128)(2,1)} %get-tuple-element.99) | copy-start | bytes 2359300
  284.7 1.8 copy-start.4
  284.7 2.5 copy-start.5
  284.7 3.1 %copy-start.3 = (f32[24,3072]{1,0:T(8,128)S(1)}, f32[24,3072]{1,0:T(8,128)}, u32[]{:S(2)}) copy-start(f32[24,3072]{1,0:T(8,128)} %get-tuple-element.109) | copy-start | bytes 884740
  285.6 2.9 %copy-start.2 = (f32[96,768]{1,0:T(8,128)S(1)}, f32[96,768]{1,0:T(8,128)}, u32[]{:S(2)}) copy-start(f32[96,768]{1,0:T(8,128)} %get-tuple-element.111) | copy-start | bytes 884740

commit v2 on v1

--- a/solution.py
+++ b/solution.py
@@ -799,8 +799,8 @@
 
 
 TN = (((0,), (0,)), ((), ()))
-BACK_ROWS = 512
-KEY_ROWS = 1024
+BACK_ROWS = 1024
+KEY_ROWS = 512
 
 
 def three(value):
@@ -829,10 +829,11 @@
 
 
 def feed_kernel(
-    length, context_rows, tok_own, cot_own, wo, small_all, wi_far, wu_far,
-    gu_far, gi_far, go_far, gs_far, output, back_context, back_residual,
-    send_sem, local_sem, sem_out, sem_back,
+    length, context_rows_far, tok_far, cot_far, wo_far, small_all, wi_far, wu_far,
+    hu_far, hi_far, ho_far, hs_far, output, back_context, back_residual,
+    send_sem, local_sem, sem1, sem2, sem_out, sem_back,
     gu, gi, go, gs, wi, back_near, vectors, inner_shift, active, back_inner, output_low,
+    r1u, r1i, r1o, r1s, r2u, context_rows, tok_own, cot_own, wo, load_sem,
 ):
     bf16, f32 = jnp.bfloat16, jnp.float32
     y, x, z, c = place()
@@ -842,17 +843,39 @@
     across = at(y, 1 - x, z, c)
     diagonal = at(y, 1 - x, z, 1 - c)
     spots = [column(lax.rem(spot + k, 8)) for k in range(1, 8)]
+    y1, x1 = jnp.where(c == 0, y, 1 - y), jnp.where(c == 0, 1 - x, x)
+    y2, x2 = jnp.where(c == 0, 1 - y, y), jnp.where(c == 0, x, 1 - x)
+    first = at(y1, x1, z, c)
+    own, near1, near2 = y * 2 + x, y1 * 2 + x1, y2 * 2 + x2
+    far = (1 - y) * 2 + 1 - x
+    order = (far, near1, near2, own)
+    parts = (gu, gi, go, gs)
+    r1 = (r1u, r1i, r1o, r1s)
     group = quad(x, c)
-    meet([at(yy, x, zz, c) for yy, zz in spots] + [across, other_core, diagonal])
     move = Mover(send_sem, local_sem, other_core)
     width = wo.shape[0]
     ff = wi.shape[1]
-    move.keep(wi_far, wi)
-    move.keep(wu_far, gu)
+    steps = ff // width
+    for source, target in ((context_rows_far, context_rows), (wo_far, wo), (tok_far, tok_own), (cot_far, cot_own)):
+        move.keep(source, target)
+
+    def weights_load(step):
+        cols = pl.ds(pl.multiple_of(step * width, width), width)
+        return (
+            pltpu.make_async_copy(wi_far.at[:, cols], wi.at[:, cols], load_sem.at[step, 0]),
+            pltpu.make_async_copy(wu_far.at[step], gu.at[step], load_sem.at[step, 1]),
+        )
+
+    def load(step, _):
+        for copy in weights_load(step):
+            copy.start()
+        return 0
+
+    lax.fori_loop(0, steps, load, 0)
+    meet([at(yy, x, zz, c) for yy, zz in spots] + [across, other_core, diagonal])
 
     piece = tok_own.shape[1]
     rows = tok_own.shape[0] * piece
-    steps = ff // width
     unpack(small_all, vectors)
     ff_piece = ff // 32
     for block in range(32):
@@ -869,6 +892,8 @@
     def square(item):
         return jnp.sum(item * item)
 
+    for n in range(4):
+        move.kept(n)
     branch = vectors[4:5, :] + dot(context_rows[0].reshape(rows, GROUP), wo[:GROUP, :])
     for g in range(1, 4):
         branch = branch + dot(context_rows[g].reshape(rows, GROUP), wo[g * GROUP : (g + 1) * GROUP, :])
@@ -881,11 +906,11 @@
     second_low = (unit * vectors[5:6, :] + vectors[6:7, :]).astype(bf16)
     back_result = jnp.where(keep, wide(cot_own[...].reshape(rows, width)), 0.0)
     back_feed = back_result.astype(bf16)
-    move.kept(0)
-    move.kept(1)
 
     def middle(step, sums_here):
         back_second, feed = sums_here
+        for copy in weights_load(step):
+            copy.wait()
         cols = pl.ds(pl.multiple_of(step * width, width), width)
         wi_here = wi[:, cols]
         inner = dot(second_low, wi_here) + inner_shift[:, cols]
@@ -934,6 +959,13 @@
     totals = (square(result), branch_total, square(jnp.where(keep, feed, 0.0)))
     lane = lax.broadcasted_iota(jnp.int32, (1, 128), 1)
     stat_row = jnp.where(lane == 0, totals[0], jnp.where(lane == 1, totals[1], jnp.where(lane == 2, totals[2], 0.0)))
+    def to_core(i, quarter):
+        move.push(parts[i].at[quarter, :, 1 - c], r1[i].at[quarter], sem1.at[i, quarter], other_core)
+
+    def gather(i, quarter):
+        move.landed(r1[i].at[quarter], sem1.at[i, quarter])
+        r1[i][quarter] = r1[i][quarter] + parts[i][quarter, :, c]
+
     lead = width // 32
     wide_piece = ff // 32
     for step in range(steps):
@@ -942,21 +974,27 @@
             for cc in range(2):
                 row = (zz * 2 + cc) * wide_piece
                 gu[step, zz, cc] = grad[row : row + wide_piece, :]
-        move.keep(gu.at[step], gu_far.at[step])
+        to_core(0, step)
     for step in range(steps):
         grad = dot(second_low, back_inner[:, step * width : (step + 1) * width], TN)
         for block in range(32):
             gi[block // 8, block % 8 // 2, block % 2, :, step * width : (step + 1) * width] = grad[
                 block * lead : (block + 1) * lead, :
             ].astype(bf16)
-    move.keep(gi, gi_far)
+    for quarter in order:
+        to_core(1, quarter)
+    for slot, quarter in ((1, far), (0, near1)):
+        gather(0, quarter)
+        move.push(r1u.at[quarter], r2u.at[slot], sem2.at[slot], first)
+    for quarter in (near2, own):
+        gather(0, quarter)
     for g in range(4):
         grad = dot(context_rows[g].reshape(rows, GROUP), back_branch, TN)
         for zz in range(4):
             for cc in range(2):
                 row = (zz * 2 + cc) * lead
                 go[g, zz, cc] = grad[row : row + lead, :].astype(bf16)
-        move.keep(go.at[g], go_far.at[g])
+        to_core(2, g)
 
     long = column_sum(wide(back_inner[...]))
     for block in range(32):
@@ -965,22 +1003,32 @@
         gs[at_block + (slice(0, 8), slice(0, lead))] = short[:, block * lead : (block + 1) * lead]
         gs[at_block + (slice(4, 5), slice(0, wide_piece))] = long[:, block * wide_piece : (block + 1) * wide_piece]
         gs[at_block + (slice(5, 6), slice(None))] = stat_row
-    move.keep(gs, gs_far)
+    for quarter in order:
+        to_core(3, quarter)
+    for i in (1, 2, 3):
+        for quarter in order:
+            gather(i, quarter)
+    for slot, quarter in ((1, near2), (0, own)):
+        move.landed(r2u.at[slot], sem2.at[slot])
+        r1u[quarter] = r1u[quarter] + r2u[slot]
+    for source, target in zip(r1, (hu_far, hi_far, ho_far, hs_far)):
+        move.keep(source, target)
     for xx, cc in group:
         for yy in range(2):
             move.landed(back_context.at[yy, xx, :, cc], sem_back.at[xx * 2 + cc, yy])
     for k in range(1, 8):
         t = lax.rem(spot + 8 - k, 8)
         move.landed(output.at[t], sem_out.at[t])
-    move.finish(range(2, len(move.local)))
+    move.finish(range(4, len(move.local)))
 
 
 def backward_kernel(
-    gu, gi, go, gs, query, key, value, context, back_context, joint_weight, first_far, tok_own, back_residual, vectors,
+    hu, hi, ho, hs, query_far, key_far, value_far, context_far, back_far, weight_far, first_far, tok_far, residual_far, vectors,
     out_o, out_i, out_u, out_s, out_joint, tokens_gradient, late,
-    send_sem, local_sem, sem1, sem2, sem3, sem4, sem_y, sem_z, sem_g, sem_c, sem_x, sem_t, sem_s,
-    r1u, r1i, r1o, r1s, r2u, r2i, r2o, r2s, r3u, r3i, r3o, r3s, r4u, r4i, r4o, r4s, ou, oi, oo, os_,
-    joint, sums, turned, first_low, back_first, rc, rx, gj, ry, rz, sj, joint_land, gradient_low, small, small_all,
+    send_sem, local_sem, sem2, sem3, sem4, sem_y, sem_z, sem_g, sem_c, sem_x, sem_t, sem_s,
+    r1u, r1i, r1o, r1s, r2u, r2i, r2o, r2s, r3u, r3i, r3o, r3s, r4u, r4i, r4o, r4s,
+    joint, back_query, widened, query, key, value, context, back_context, joint_weight, tok_own, back_residual,
+    first_low, back_first, rc, rx, gj, ry, rz, sj, joint_land, gradient_low, small, small_all,
 ):
     bf16, f32 = jnp.bfloat16, jnp.float32
     y, x, z, c = place()
@@ -1003,48 +1051,48 @@
     for k in range(1, 32):
         t = lax.rem(me + k, 32)
         others.append((t, (t // 8, lax.rem(t, 8))))
+    move = Mover(send_sem, local_sem, other_core)
+    move.keep(back_far, back_context)
+    move.keep(context_far, context)
+    for h in range(3):
+        for source, target in ((key_far, key), (query_far, query), (value_far, value)):
+            move.keep(source.at[h], target.at[h])
     meet([device for _, device in others])
-    move = Mover(send_sem, local_sem, other_core)
     zero = move.zero
-    parts = (gu, gi, go, gs)
-    halves = (ou, oi, oo, os_)
+    sources = (hu, hi, ho, hs)
     results = (out_u, out_i, out_o, out_s)
     r1, r2 = (r1u, r1i, r1o, r1s), (r2u, r2i, r2o, r2s)
     r3, r4 = (r3u, r3i, r3o, r3s), (r4u, r4i, r4o, r4s)
-    for i in (0, 2, 3, 1):
-        for quarter in order:
-            move.push(
-                parts[i].at[quarter, :, 1 - c], r1[i].at[quarter], sem1.at[i, quarter], other_core
-            )
     for i in range(4):
-        move.keep(parts[i].at[:, :, c], halves[i])
-    move.keep(first_far, first_low)
-
-    def gather(i, quarter):
-        move.landed(r1[i].at[quarter], sem1.at[zero + i, quarter])
-        r1[i][quarter] = (wide(r1[i][quarter]) + wide(halves[i][quarter])).astype(r1[i].dtype)
+        move.keep(sources[i], r1[i])
+    for source, target in (
+        (weight_far, joint_weight), (first_far, first_low), (tok_far, tok_own), (residual_far, back_residual)
+    ):
+        move.keep(source, target)
 
     def stage2(i):
         for slot, quarter in ((1, far), (0, near1)):
-            gather(i, quarter)
             move.push_made(
                 lambda slot=slot, quarter=quarter: (
-                    r1[i].at[quarter], r2[i].at[zero + slot], sem2.at[zero + i, zero + slot]
+                    sources[i].at[quarter], r2[i].at[zero + slot], sem2.at[zero + i, zero + slot]
                 ),
                 first,
             )
 
     def stage3(i):
-        gather(i, near2)
-        move.landed(r2[i].at[zero + 1], sem2.at[zero + i, zero + 1])
-        r1[i][near2] = (wide(r1[i][near2]) + wide(r2[i][1])).astype(r1[i].dtype)
-        move.push_made(lambda: (r1[i].at[near2], r3[i], sem3.at[zero + i]), second)
+        if i:
+            move.landed(r2[i].at[zero + 1], sem2.at[zero + i, zero + 1])
+            r1[i][near2] = r1[i][near2] + r2[i][1]
+        source = r1[i] if i else sources[i]
+        move.push_made(lambda: (source.at[near2], r3[i], sem3.at[zero + i]), second)
 
     def stage4(i):
-        gather(i, own)
-        move.landed(r2[i].at[zero], sem2.at[zero + i, zero])
+        total = wide(r1[i][own])
+        if i:
+            move.landed(r2[i].at[zero], sem2.at[zero + i, zero])
+            total = total + wide(r2[i][0])
         move.landed(r3[i], sem3.at[zero + i])
-        r1[i][own] = (wide(r1[i][own]) + wide(r2[i][0]) + wide(r3[i][...])).astype(r1[i].dtype)
+        r1[i][own] = (total + wide(r3[i][...])).astype(r1[i].dtype)
         for k in range(3):
             move.push_made(
                 lambda k=k: (r1[i].at[own, line[k]], r4[i].at[zero + k], sem4.at[zero + i, zero + k]),
@@ -1064,68 +1112,71 @@
     width = tok_own.shape[2]
     scale = DH ** (-0.5)
     eye = jnp.eye(DH, 2 * DH, dtype=bf16)
-    side_lane = lax.broadcasted_iota(jnp.int32, (BACK_ROWS, DH), 1)
-    per_head = rows_all // BACK_ROWS
+    side_lane = lax.broadcasted_iota(jnp.int32, (rows, DH), 1)
+    per_head = rows_all // KEY_ROWS
     between = {
-        1: lambda: stage2(0),
-        2: lambda: (stage2(2), stage2(3)),
-        3: lambda: stage2(1),
-        6: lambda: stage3(0),
-        7: lambda: (stage3(2), stage3(3)),
-        9: lambda: stage4(0),
-        10: lambda: (stage4(2), stage4(3)),
-        11: lambda: stage3(1),
+        0: lambda: (stage4(0), stage3(2), stage3(3)),
+        1: lambda: (stage3(1), stage4(2), stage4(3)),
+        2: lambda: None,
     }
-    for n in range(4):
-        move.kept(n)
+    stage3(0)
+    stage2(2)
+    stage2(3)
+    stage2(1)
+    move.kept(0)
+    move.kept(1)
     for h in range(3):
-        for k in range(rows_all // KEY_ROWS):
-            turned[k] = dot(eye, key[h, k * KEY_ROWS : (k + 1) * KEY_ROWS, :], NT).astype(bf16)
-        sums[...] = jnp.zeros_like(sums)
+        for n in range(3):
+            move.kept(2 + 3 * h + n)
+        if h == 0:
+            for n in range(11, 15):
+                move.kept(n)
         lanes = slice(h * DH, (h + 1) * DH)
-
-        def block(i, _):
-            here = pl.ds(i * BACK_ROWS, BACK_ROWS)
-            queries = query[h, here, :]
-            backs = back_context[i // 2, lax.rem(i, 2)].reshape(BACK_ROWS, GROUP)[:, lanes]
+        for q in range(4):
+            here = slice(q * rows, (q + 1) * rows)
+            backs = back_context[q // 2, q % 2].reshape(rows, GROUP)[:, lanes]
             spread = jnp.sum(wide(backs) * wide(context[here, lanes]), axis=1, keepdims=True)
             high, mid, low = three(spread)
             side = jnp.where(
                 side_lane == 0, -high, jnp.where(side_lane == 1, -mid, jnp.where(side_lane == 2, -low, 0.0))
             )
-            widened = jnp.concatenate([backs, side.astype(bf16)], axis=1)
-
-            def part(k, back_query):
-                keys = pl.ds(k * KEY_ROWS, KEY_ROWS)
-                chances = jnp.exp(dot(key[h, keys, :], queries, NT))
-                back_scores = (chances * dot(value[h, keys, :], widened, NT)).astype(bf16)
-                sums[keys, :DH] += dot(back_scores, queries[:, :DH])
-                sums[keys, DH:] += dot(chances.astype(bf16), backs)
-                return back_query + dot(turned[k], back_scores)
-
-            back_query = jnp.zeros((DH, BACK_ROWS), f32)
-            back_query = lax.fori_loop(0, rows_all // KEY_ROWS, part, back_query)
-            joint[here, lanes] = (back_query * scale).T.astype(bf16)
-            for step, action in between.items():
-                if step // per_head == h:
-
-                    @pl.when(i == step % per_head)
-                    def _(action=action):
-                        action()
-
+            widened[here, :] = jnp.concatenate([backs, side.astype(bf16)], axis=1)
+        back_query[...] = jnp.zeros_like(back_query)
+
+        def block(i, _):
+            keys = pl.ds(i * KEY_ROWS, KEY_ROWS)
+            key_here, value_here = key[h, keys, :], value[h, keys, :]
+            turned = dot(eye, key_here, NT).astype(bf16)
+            back_key = jnp.zeros((KEY_ROWS, DH), f32)
+            back_value = jnp.zeros((KEY_ROWS, DH), f32)
+            for q in range(rows_all // BACK_ROWS):
+                here = slice(q * BACK_ROWS, (q + 1) * BACK_ROWS)
+                queries, backs = query[h, here, :], widened[here, :]
+                chances = jnp.exp(dot(key_here, queries, NT))
+                back_scores = (chances * dot(value_here, backs, NT)).astype(bf16)
+                back_key = back_key + dot(back_scores, queries[:, :DH])
+                back_value = back_value + dot(chances.astype(bf16), backs[:, :DH])
+                back_query[:, here] += dot(turned, back_scores)
+            joint[keys, GROUP + h * DH : GROUP + (h + 1) * DH] = back_key.astype(bf16)
+            joint[keys, 2 * GROUP + h * DH : 2 * GROUP + (h + 1) * DH] = back_value.astype(bf16)
             return 0
 
         lax.fori_loop(0, per_head, block, 0)
-        joint[:, GROUP + h * DH : GROUP + (h + 1) * DH] = sums[:, :DH].astype(bf16)
-        joint[:, 2 * GROUP + h * DH : 2 * GROUP + (h + 1) * DH] = sums[:, DH:].astype(bf16)
-
+        joint[:, lanes] = (back_query[...] * scale).T.astype(bf16)
+        between[h]()
+
+    move.kept(15)
     for k in range(2):
         for yy in range(2):
             xx = lax.rem(x + 1 + k, 2)
             here = pl.ds((yy * 2 + xx) * rows, rows)
             back_first[yy, xx] = dot(joint[here, :], joint_weight[...], NT).astype(bf16).reshape(4, 2, piece, width)
             move.push(back_first.at[yy, xx, :, 1 - c], rc.at[yy, xx], sem_c.at[yy, xx], other_core)
-    move.kept(4)
+    for yy in range(2):
+        move.landed(rc.at[yy, 1 - x], sem_c.at[yy, 1 - x])
+        rc[yy, 1 - x] = rc[yy, 1 - x] + back_first[yy, 1 - x, :, c]
+        move.push(rc.at[yy, 1 - x], rx.at[yy], sem_x.at[yy], across)
+    move.kept(16)
     grad = dot(first_low[...], joint[...], TN)
     lead = width // 32
     for block_at in range(32):
@@ -1133,10 +1184,8 @@
             block_at * lead : (block_at + 1) * lead, :
         ].astype(bf16)
     move.push(gj.at[1 - y], ry, sem_y, down)
-    for yy in range(2):
-        move.landed(rc.at[yy, 1 - x], sem_c.at[yy, 1 - x])
-        rc[yy, 1 - x] = (wide(rc[yy, 1 - x]) + wide(back_first[yy, 1 - x, :, c])).astype(bf16)
-        move.push(rc.at[yy, 1 - x], rx.at[yy], sem_x.at[yy], across)
+    move.kept(17)
+    move.kept(18)
     stage4(1)
     shifts = jnp.sum(wide(joint[...]), axis=0, keepdims=True)
     small[...] = jnp.zeros_like(small)
@@ -1145,32 +1194,39 @@
             start = kind * GROUP + k * lead
             small[mine * 8 + k, row : row + 1, :lead] = shifts[:, start : start + lead]
     move.landed(ry, sem_y)
-    ry[...] = (wide(ry[...]) + wide(gj[y])).astype(bf16)
+    ry[...] = ry[...] + gj[y]
     for k in range(3):
         move.push(ry.at[:, line[k]], rz.at[k], sem_z.at[k], line_devices[k])
     for yy in range(2):
         move.landed(rc.at[yy, x], sem_c.at[yy, x])
 
-    inputs = wide(tok_own[...].reshape(rows, width))
-    centered = inputs - mean_of(inputs)
-    inverse = lax.rsqrt(mean_of(centered * centered) + EPS)
-    unit = centered * inverse
-    halves_rows = []
+    kept = []
+    gains = jnp.zeros((2, width), f32)
+    half = rows // 2
     for yy in range(2):
+        inputs = wide(tok_own[yy * 4 : yy * 4 + 4].reshape(half, width))
+        centered = inputs - mean_of(inputs)
+        inverse = lax.rsqrt(mean_of(centered * centered) + EPS)
+        unit = centered * inverse
         move.landed(rx.at[yy], sem_x.at[yy])
         whole = wide(rc[yy, x]) + wide(back_first[yy, x, :, c]) + wide(rx[yy])
-        halves_rows.append(whole.reshape(rows // 2, width))
-    back_one = jnp.concatenate(halves_rows, axis=0)
-    scaled = back_one * vectors[0:1, :]
-    back_tokens = back_residual[...] + inverse * (scaled - mean_of(scaled) - unit * mean_of(scaled * unit))
-    gradient_low[...] = back_tokens.astype(bf16).reshape(8, piece, width)
-    for k in range(1, 8):
-        yy, zz = column(lax.rem(spot + k, 8))
-        move.push(gradient_low.at[yy * 4 + zz], tokens_gradient.at[spot], sem_t.at[spot], at(yy, x, zz, c))
-    kept = [move.keep(gradient_low.at[spot], tokens_gradient.at[spot])]
-    gains = jnp.concatenate(
-        [jnp.sum(back_one * unit, axis=0, keepdims=True), jnp.sum(back_one, axis=0, keepdims=True)], axis=0
-    )
+        back_one = whole.reshape(half, width)
+        scaled = back_one * vectors[0:1, :]
+        back_tokens = back_residual[yy * half : (yy + 1) * half, :] + inverse * (
+            scaled - mean_of(scaled) - unit * mean_of(scaled * unit)
+        )
+        gradient_low[yy * 4 : yy * 4 + 4] = back_tokens.astype(bf16).reshape(4, piece, width)
+        for zz in [lax.rem(z + k, 4) for k in range(4)]:
+            there = y * 0 + yy
+            move.push_made(
+                lambda zz=zz, yy=yy: (gradient_low.at[yy * 4 + zz], tokens_gradient.at[spot], sem_t.at[spot]),
+                at(there, x, zz, c),
+                jnp.logical_or(y != yy, z != zz),
+            )
+        gains = gains + jnp.concatenate(
+            [jnp.sum(back_one * unit, axis=0, keepdims=True), jnp.sum(back_one, axis=0, keepdims=True)], axis=0
+        )
+    kept.append(move.keep(gradient_low.at[spot], tokens_gradient.at[spot]))
     for block_at in range(32):
         small[block_at, 0:2, :lead] = gains[:, block_at * lead : (block_at + 1) * lead]
     for t, device in others:
@@ -1295,9 +1351,9 @@
         (output_weight.shape, bf16),
         ((8, 128), f32),
     ]
-    gu, gi, go, gs, output, back_context, back_residual = comm_call(
+    hu, hi, ho, hs, output, back_context, back_residual = comm_call(
         feed_kernel,
-        [(grid + shape, dtype, hbm) for shape, dtype in kinds]
+        [((4, 4) + shape, dtype, hbm) for shape, dtype in kinds]
         + [
             (tokens.shape, bf16, hbm),
             (natural + (GROUP,), bf16, vmem),
@@ -1307,7 +1363,7 @@
             length, context_rows.reshape(4, 8, piece, GROUP), tok_own, cot_own, wo_all.reshape(width, width), small_all,
             wi_all.reshape(width, ff), wu_all.reshape(grid + outer_weight.shape),
         ),
-        20, 20, [(8,), (4, 2)],
+        48, 24, [(4, 4), (2,), (8,), (4, 2)],
         [vmem(grid + shape, dtype) for shape, dtype in kinds]
         + [
             vmem((width, ff), bf16),
@@ -1317,9 +1373,18 @@
             vmem((rows, ff), bf16),
             vmem((rows, ff), bf16),
             vmem((8, piece, width), bf16),
+        ]
+        + [vmem((4, 4) + shape, dtype) for shape, dtype in kinds]
+        + [
+            vmem((2, 4) + outer_weight.shape, bf16),
+            vmem((4, 8, piece, GROUP), bf16),
+            vmem((8, piece, width), bf16),
+            vmem((8, piece, width), bf16),
+            vmem((width, width), bf16),
+            dma((4, 2)),
         ],
         1,
-        [pltpu.SMEM] + [vmem] * 5 + [hbm] * 2,
+        [pltpu.SMEM] + [hbm] * 4 + [vmem] + [hbm] * 2,
     )
     out_o, out_i, out_u, out_s, joint_shard, tokens_gradient, late = comm_call(
         backward_kernel,
@@ -1333,19 +1398,26 @@
             ((8, 128), f32, vmem),
         ],
         (
-            gu, gi, go, gs, query, key, value, context, back_context, joint_here, first_low, tok_own, back_residual, vectors,
+            hu, hi, ho, hs, query, key, value, context, back_context, joint_here, first_low, tok_own, back_residual, vectors,
         ),
-        110, 16,
-        [(4, 4), (4, 2), (4,), (4, 3), (), (3,), (4,), (2, 2), (2,), (8,), (32,)],
+        110, 32,
+        [(4, 2), (4,), (4, 3), (), (3,), (4,), (2, 2), (2,), (8,), (32,)],
         [vmem((4, 4) + shape, dtype) for shape, dtype in kinds]
         + [vmem((2, 4) + shape, dtype) for shape, dtype in kinds]
         + [vmem((4,) + shape, dtype) for shape, dtype in kinds]
         + [vmem((3,) + shape, dtype) for shape, dtype in kinds]
-        + [vmem((4, 4) + shape, dtype) for shape, dtype in kinds]
         + [
             vmem((rows_all, 3 * GROUP), bf16),
-            vmem((rows_all, 2 * DH), f32),
-            vmem((rows_all // KEY_ROWS, DH, KEY_ROWS), bf16),
+            vmem((DH, rows_all), f32),
+            vmem((rows_all, 2 * DH), bf16),
+            vmem(query.shape, bf16),
+            vmem(key.shape, bf16),
+            vmem(value.shape, bf16),
+            vmem(context.shape, bf16),
+            vmem(back_context.shape, bf16),
+            vmem(joint_here.shape, bf16),
+            vmem(tok_own.shape, bf16),
+            vmem(back_residual.shape, f32),
             vmem((rows_all, width), bf16),
             vmem(natural + (width,), bf16),
             vmem((2, 2, 4, piece, width), bf16),
@@ -1360,7 +1432,7 @@
             vmem((32, 8, 128), f32),
         ],
         2,
-        [hbm] * 4 + [vmem] * 6 + [hbm] + [vmem] * 3,
+        [hbm] * 13 + [vmem],
     )
     count = jnp.sum(lengths).astype(f32) * width
     stats = jnp.sqrt(out_s[5, :3] / count + 1e-06)

time: 295 us -> 285 us (0.966)
  Pallas kernels: 272 us -> 261 us
    pallas_call x3, Pallas kernels: 272 us -> 261 us  [comm_call(): pl.pallas_call(kernel, out_shape=[jax.ShapeDtypeStruct(shape, dtype) for...]
where the time goes in v2:
time: 285 us; the launch traced here: 280 us
  Pallas kernels  261 us (92%)
  local copies, waits for them, and re-layouts  13.6 us (5%)
  other arithmetic  3.28 us (1%)
    pallas_call x3, Pallas kernels, comm_call(): pl.pallas_call(kernel, out_shape=[jax.ShapeDtypeStruct(shape, dtype) for...  261 us
    unnamed x18, local copies, waits for them, and re-layouts  5.71 us

profile of v2, /device:TPU:0, one launch (start us, length us, event | category | flops | bytes accessed | tf_op | source)
XLA Modules:
  0.0 280.0 jit_solution(7077844425033899767)
XLA Ops:
  0.7 1.2 dynamic_slice.3.length
  1.9 1.1 reshape.58
  3.0 0.1 copy.37
  3.1 0.8 reshape.59.wj
  3.9 0.7 broadcast_in_dim.3
  4.5 0.8 stack.35
  5.3 0.6 fusion.1.small
  5.9 110.9 %shard_map.279 = (bf16[2048,768]{1,0:T(8,128)(2,1)}, bf16[3,2048,128]{2,1,0:T(8,128)(2,1)}, bf16[3,2048,128]{2,1,0:T(8,128)(2,1)}, bf16[3,2048,128]{2,1,0:T(8,12...) custom-call(s32[1]{0:T(128)} %dynamic_slice.3.length, ...), custom_call_target="tpu_custom_call" | custom-call | tf_op jit(solution)/shard_map/pallas_call | solution.py:769
  116.9 51.6 %shard_map.280 = (bf16[4,4,96,768]{3,2,1,0:T(8,128)(2,1)}, bf16[4,4,24,3072]{3,2,1,0:T(8,128)(2,1)}, bf16[4,4,24,768]{3,2,1,0:T(8,128)(2,1)}, f32[4,4,8,128]{3,2...) custom-call(s32[1]{0:T(128)} %dynamic_slice.3.length, ...), custom_call_target="tpu_custom_call" | custom-call | tf_op jit(solution)/shard_map/pallas_call | solution.py:769
  168.5 0.9 convert_bitcast_fusion
  169.4 0.7 reshape.64.vectors
  170.1 0.0 copy-start.5
  170.1 0.0 copy-start
  170.1 98.7 %shard_map.281 = (f32[24,768]{1,0:T(8,128)}, f32[24,3072]{1,0:T(8,128)}, f32[96,768]{1,0:T(8,128)}, f32[8,128]{1,0:T(8,128)}, f32[24,2304]{1,0:T(8,128)}, /*index=5*/bf16[8,64,768]{2,1,0:T(8,128)(2,1)}, f32[8,128]{1,0:T(8,128)}) custom-call(bf16[4,4,96,768]{3,2,1,0:T(8,128)(2,1)} %get-tuple-element.51.hu, bf16[4,4,24,3072]{3,2,1,0:T(8,128)(2,1)} %get-tuple-element.52.hi, ...), custom_call_target="tpu_custom_call" | custom-call | tf_op jit(solution)/shard_map/pallas_call | solution.py:769
  268.8 0.0 copy-start.3
  268.8 0.0 copy-start.4
  268.8 0.0 copy-start.2
  268.8 0.0 copy-start.1
  268.8 1.4 slice_bitcast_fusion
  270.2 0.0 copy-done.5
  270.2 0.6 reduce_sum.9
  271.5 1.2 sqrt_bitcast_fusion
  272.7 1.2 slice_bitcast_fusion.1
  273.9 0.0 copy-done
  273.9 0.9 copy.44
  274.7 2.1 copy.45
  276.8 0.0 copy-done.3
  276.8 0.7 copy.46
  277.5 0.0 copy-done.4
  277.5 0.6 copy.47
  278.1 0.0 copy-done.2
  278.1 0.7 copy.48
  278.9 0.0 copy-done.1
  278.9 0.7 copy.49
  (1 shorter events, 0.0 us)
Async XLA Ops:
  170.1 100.1 %copy-start.5 = (s32[8]{0:T(128)S(1)}, s32[8]{0:T(128)}, u32[]{:S(2)}) copy-start(s32[8]{0:T(128)} %param.17) | copy-start | bytes 100
  170.1 103.8 %copy-start = (bf16[8,64,768]{2,1,0:T(8,128)(2,1)S(1)}, bf16[8,64,768]{2,1,0:T(8,128)(2,1)}, u32[]{:S(2)}) copy-start(bf16[8,64,768]{2,1,0:T(8,128)(2,1)} %get-tuple-element.98) | copy-start | bytes 2359300
  268.8 8.0 %copy-start.3 = (f32[24,2304]{1,0:T(8,128)S(1)}, f32[24,2304]{1,0:T(8,128)}, u32[]{:S(2)}) copy-start(f32[24,2304]{1,0:T(8,128)} %get-tuple-element.102) | copy-start | bytes 663556
  268.8 8.7 %copy-start.4 = (f32[24,768]{1,0:T(8,128)S(1)}, f32[24,768]{1,0:T(8,128)}, u32[]{:S(2)}) copy-start(f32[24,768]{1,0:T(8,128)} %get-tuple-element.105) | copy-start | bytes 221188
  268.8 9.3 %copy-start.2 = (f32[24,3072]{1,0:T(8,128)S(1)}, f32[24,3072]{1,0:T(8,128)}, u32[]{:S(2)}) copy-start(f32[24,3072]{1,0:T(8,128)} %get-tuple-element.109) | copy-start | bytes 884740
  268.8 10.1 %copy-start.1 = (f32[96,768]{1,0:T(8,128)S(1)}, f32[96,768]{1,0:T(8,128)}, u32[]{:S(2)}) copy-start(f32[96,768]{1,0:T(8,128)} %get-tuple-element.111) | copy-start | bytes 884740

commit v3 on v2

--- a/solution.py
+++ b/solution.py
@@ -469,9 +469,9 @@
 
 def forward_kernel(
     length, tokens, cotangent, wj, wo, wi, wu, small,
-    first_far, query_far, key_far, value_far, context, context_rows, cot_own, tok_own, wo_all, wi_all, wu_all, small_all, wj_flat,
+    first_far, query_far, key_far, value_far, context_far, context_rows, cot_own, tok_own, wo_all, wi_all, wu_all, small_all, wj_far, vectors,
     send_sem, local_sem, tok_sem, cot_sem, weight_sem, small_sem, wja_sem, wjb_sem, wjc_sem, ctx_send, ctx_recv,
-    ctx_local, tok_all, wj_all, vectors, turned, mixed_low, score_a, score_b, straight_low, first_low, query, key, value,
+    ctx_local, tok_all, wj_all, turned, mixed_low, score_a, score_b, straight_low, first_low, query, key, value, context, wj_flat,
 ):
     y, x, z, c = place()
     mine = number(y, x, z, c)
@@ -640,7 +640,7 @@
         low_q = ((joint[:, :GROUP] + query_shift).astype(jnp.bfloat16) * DH ** (-0.5)).astype(jnp.bfloat16)
         low_k = joint[:, GROUP : 2 * GROUP].astype(jnp.bfloat16)
         low_v = (joint[:, 2 * GROUP :] + value_shift).astype(jnp.bfloat16)
-        mask = jnp.where(row_at + i * ROWS < length[0], 0.0, NEG)
+        mask = jnp.where(row_at + i * ROWS < length[spot], 0.0, NEG)
         key_side = jnp.where(lane == 0, mask, jnp.where(lane < 4, 1.0, 0.0)).astype(jnp.bfloat16)
         for h in range(3):
             here_h = slice(h * DH, (h + 1) * DH)
@@ -651,7 +651,7 @@
 
     for i in range(rows // ROWS):
         project(i, 0)
-    for source, target in ((first_low, first_far), (key, key_far), (value, value_far)):
+    for source, target in ((first_low, first_far), (key, key_far), (value, value_far), (wj_flat, wj_far)):
         move.keep(source, target)
     eye = jnp.eye(72, 2 * DH, dtype=jnp.bfloat16)
     for h in range(3):
@@ -738,6 +738,7 @@
 
     lax.fori_loop(0, units // 2, pair, start)
     move.keep(query, query_far)
+    move.keep(context, context_far)
     last_hand(2)
     last_hand(3)
     for yy, zz in back_spots:
@@ -829,10 +830,10 @@
 
 
 def feed_kernel(
-    length, context_rows_far, tok_far, cot_far, wo_far, small_all, wi_far, wu_far,
+    length, context_rows_far, tok_far, cot_far, wo_far, small_all, vectors, wi_far, wu_far,
     hu_far, hi_far, ho_far, hs_far, output, back_context, back_residual,
     send_sem, local_sem, sem1, sem2, sem_out, sem_back,
-    gu, gi, go, gs, wi, back_near, vectors, inner_shift, active, back_inner, output_low,
+    gu, gi, go, gs, wi, back_near, inner_shift, active, back_inner, output_low,
     r1u, r1i, r1o, r1s, r2u, context_rows, tok_own, cot_own, wo, load_sem,
 ):
     bf16, f32 = jnp.bfloat16, jnp.float32
@@ -876,7 +877,6 @@
 
     piece = tok_own.shape[1]
     rows = tok_own.shape[0] * piece
-    unpack(small_all, vectors)
     ff_piece = ff // 32
     for block in range(32):
         inner_shift[:, block * ff_piece : (block + 1) * ff_piece] = wide(small_all[block])[8:9, :ff_piece]
@@ -884,7 +884,7 @@
     spot_at = lax.broadcasted_iota(jnp.int32, (8, piece, 1), 0)
     position = number(spot_at // 4, x, lax.rem(spot_at, 4), c) * piece
     position = position + lax.broadcasted_iota(jnp.int32, (8, piece, 1), 1)
-    keep = jnp.where(position < length[0], 1.0, 0.0).reshape(rows, 1) > 0.5
+    keep = jnp.where(position < length[spot], 1.0, 0.0).reshape(rows, 1) > 0.5
 
     def column_sum(item):
         return jnp.sum(item, axis=0, keepdims=True)
@@ -1211,6 +1211,15 @@
         move.landed(rx.at[yy], sem_x.at[yy])
         whole = wide(rc[yy, x]) + wide(back_first[yy, x, :, c]) + wide(rx[yy])
         back_one = whole.reshape(half, width)
+        gains = gains + jnp.concatenate(
+            [jnp.sum(back_one * unit, axis=0, keepdims=True), jnp.sum(back_one, axis=0, keepdims=True)], axis=0
+        )
+        if yy == 1:
+            for block_at in range(32):
+                small[block_at, 0:2, :lead] = gains[:, block_at * lead : (block_at + 1) * lead]
+            for t, device in others:
+                move.push(small.at[t], small_all.at[me], sem_s.at[me], device)
+            kept.append(move.keep(small.at[me], small_all.at[me]))
         scaled = back_one * vectors[0:1, :]
         back_tokens = back_residual[yy * half : (yy + 1) * half, :] + inverse * (
             scaled - mean_of(scaled) - unit * mean_of(scaled * unit)
@@ -1223,15 +1232,7 @@
                 at(there, x, zz, c),
                 jnp.logical_or(y != yy, z != zz),
             )
-        gains = gains + jnp.concatenate(
-            [jnp.sum(back_one * unit, axis=0, keepdims=True), jnp.sum(back_one, axis=0, keepdims=True)], axis=0
-        )
     kept.append(move.keep(gradient_low.at[spot], tokens_gradient.at[spot]))
-    for block_at in range(32):
-        small[block_at, 0:2, :lead] = gains[:, block_at * lead : (block_at + 1) * lead]
-    for t, device in others:
-        move.push(small.at[t], small_all.at[me], sem_s.at[me], device)
-    kept.append(move.keep(small.at[me], small_all.at[me]))
 
     total = wide(ry[:, z])
     for k in range(3):
@@ -1300,14 +1301,13 @@
     dma, regular = pltpu.SemaphoreType.DMA, pltpu.SemaphoreType.REGULAR
     rows_all = 32 * piece
     natural = (2, 2, 4, 2, piece)
-    length = lax.dynamic_slice(lengths, (y * 4 + z,), (1,))
     joint_four = jnp.transpose(joint_weight.reshape(lead, 3, 4, GROUP), (2, 0, 1, 3)).reshape(4, lead, 3 * GROUP)
     forward_outs = [
         ((rows_all, width), bf16, hbm),
         ((3, rows_all, 2 * DH), bf16, hbm),
         ((3, rows_all, 2 * DH), bf16, hbm),
         ((3, rows_all, 2 * DH), bf16, hbm),
-        ((rows_all, GROUP), bf16, vmem),
+        ((rows_all, GROUP), bf16, hbm),
         ((4, 2, 4, piece, GROUP), bf16, vmem),
         ((8, piece, width), bf16, hbm),
         ((8, piece, width), bf16, hbm),
@@ -1315,20 +1315,20 @@
         ((32,) + inner_weight.shape, bf16, hbm),
         ((32,) + outer_weight.shape, bf16, hbm),
         ((32,) + small.shape, bf16, vmem),
-        ((width, 3 * GROUP), bf16, vmem),
+        ((width, 3 * GROUP), bf16, hbm),
+        ((8, width), f32, vmem),
     ]
     (
-        first_low, query, key, value, context, context_rows, cot_own, tok_own, wo_all, wi_all, wu_all, small_all, joint_here
+        first_low, query, key, value, context, context_rows, cot_own, tok_own, wo_all, wi_all, wu_all, small_all, joint_here, vectors
     ) = comm_call(
         forward_kernel,
         forward_outs,
-        (length, tokens, cotangent, joint_four, output_weight, inner_weight, outer_weight, small),
+        (lengths, tokens, cotangent, joint_four, output_weight, inner_weight, outer_weight, small),
         220, 24,
         [(32,), (8,), (3, 32), (32,), (4,), (4,), (4,), (4, 2), (4, 4), (4,)],
         [
             vmem((32, piece, width), bf16),
             vmem((2, 2, 4, 2, lead, 3 * GROUP), bf16),
-            vmem((8, width), f32),
             vmem((3, 72, rows_all), bf16),
             vmem(natural + (GROUP,), bf16),
             vmem((rows_all, 512), f32),
@@ -1338,11 +1338,12 @@
             vmem((3, rows_all, 2 * DH), bf16),
             vmem((3, rows_all, 2 * DH), bf16),
             vmem((3, rows_all, 2 * DH), bf16),
+            vmem((rows_all, GROUP), bf16),
+            vmem((width, 3 * GROUP), bf16),
         ],
         0,
         [pltpu.SMEM, hbm, hbm, hbm, hbm, hbm, hbm, hbm],
     )
-    vectors = jnp.transpose(small_all[:, :2, :lead], (1, 0, 2)).reshape(2, width).astype(f32)
     rows = 8 * piece
     grid = (4, 4, 2)
     kinds = [
@@ -1360,7 +1361,7 @@
             ((rows, width), f32, vmem),
         ],
         (
-            length, context_rows.reshape(4, 8, piece, GROUP), tok_own, cot_own, wo_all.reshape(width, width), small_all,
+            lengths, context_rows.reshape(4, 8, piece, GROUP), tok_own, cot_own, wo_all.reshape(width, width), small_all, vectors,
             wi_all.reshape(width, ff), wu_all.reshape(grid + outer_weight.shape),
         ),
         48, 24, [(4, 4), (2,), (8,), (4, 2)],
@@ -1368,7 +1369,6 @@
         + [
             vmem((width, ff), bf16),
             vmem((4, 8, piece, GROUP), bf16),
-            vmem((8, width), f32),
             vmem((1, ff), f32),
             vmem((rows, ff), bf16),
             vmem((rows, ff), bf16),
@@ -1384,7 +1384,7 @@
             dma((4, 2)),
         ],
         1,
-        [pltpu.SMEM] + [hbm] * 4 + [vmem] + [hbm] * 2,
+        [pltpu.SMEM] + [hbm] * 4 + [vmem] * 2 + [hbm] * 2,
     )
     out_o, out_i, out_u, out_s, joint_shard, tokens_gradient, late = comm_call(
         backward_kernel,

time: 285 us -> 279 us (0.979)
  the two profiles are of different devices: /device:TPU:0 before, /device:TPU:12 now
where the time goes in v3:
time: 279 us; the launch traced here: 274 us
  Pallas kernels  258 us (92%)
  local copies, waits for them, and re-layouts  11.7 us (4%)
    pallas_call x3, Pallas kernels, comm_call(): pl.pallas_call(kernel, out_shape=[jax.ShapeDtypeStruct(shape, dtype) for...  258 us
    unnamed x18, local copies, waits for them, and re-layouts  5.71 us

profile of v3, /device:TPU:12, one launch (start us, length us, event | category | flops | bytes accessed | tf_op | source)
XLA Modules:
  0.0 273.6 jit_solution(6221621343019324443)
XLA Ops:
  0.6 1.1 reshape.55
  1.7 0.1 copy.35
  1.8 0.8 reshape.56.wj
  2.6 0.7 broadcast_in_dim.3
  3.3 0.8 stack.35
  4.1 0.6 fusion.1.small
  4.7 101.1 %shard_map.279 = (bf16[2048,768]{1,0:T(8,128)(2,1)}, bf16[3,2048,128]{2,1,0:T(8,128)(2,1)}, bf16[3,2048,128]{2,1,0:T(8,128)(2,1)}, bf16[3,2048,128]{2,1,0:T(8,12...) custom-call(s32[8]{0:T(128)} %length.3, ...), custom_call_target="tpu_custom_call" | custom-call | tf_op jit(solution)/shard_map/pallas_call | solution.py:770
  105.7 57.4 %shard_map.280 = (bf16[4,4,96,768]{3,2,1,0:T(8,128)(2,1)}, bf16[4,4,24,3072]{3,2,1,0:T(8,128)(2,1)}, bf16[4,4,24,768]{3,2,1,0:T(8,128)(2,1)}, f32[4,4,8,128]{3,2...) custom-call(s32[8]{0:T(128)} %length.3, ...), custom_call_target="tpu_custom_call" | custom-call | tf_op jit(solution)/shard_map/pallas_call | solution.py:770
  163.1 0.0 copy-start.5
  163.1 0.0 copy-start
  163.1 99.2 %shard_map.281 = (f32[24,768]{1,0:T(8,128)}, f32[24,3072]{1,0:T(8,128)}, f32[96,768]{1,0:T(8,128)}, f32[8,128]{1,0:T(8,128)}, f32[24,2304]{1,0:T(8,128)}, /*index=5*/bf16[8,64,768]{2,1,0:T(8,128)(2,1)}, f32[8,128]{1,0:T(8,128)}) custom-call(bf16[4,4,96,768]{3,2,1,0:T(8,128)(2,1)} %get-tuple-element.53.hu, bf16[4,4,24,3072]{3,2,1,0:T(8,128)(2,1)} %get-tuple-element.54.hi, ...), custom_call_target="tpu_custom_call" | custom-call | tf_op jit(solution)/shard_map/pallas_call | solution.py:770
  262.3 0.0 copy-start.3
  262.3 0.0 copy-start.4
  262.3 0.0 copy-start.2
  262.4 0.0 copy-start.1
  262.4 1.4 slice_bitcast_fusion
  263.7 0.0 copy-done.5
  263.7 0.6 reduce_sum.9
  265.0 1.2 sqrt_bitcast_fusion
  266.2 1.2 slice_bitcast_fusion.1
  267.4 0.0 copy-done
  267.4 0.9 copy.42
  268.3 2.1 copy.43
  270.4 0.0 copy-done.3
  270.4 0.7 copy.44
  271.0 0.0 copy-done.4
  271.1 0.6 copy.45
  271.7 0.0 copy-done.2
  271.7 0.7 copy.46
  272.4 0.0 copy-done.1
  272.4 0.7 copy.47
Async XLA Ops:
  163.1 100.6 %copy-start.5 = (s32[8]{0:T(128)S(1)}, s32[8]{0:T(128)}, u32[]{:S(2)}) copy-start(s32[8]{0:T(128)} %length.3) | copy-start | bytes 100
  163.1 104.3 %copy-start = (bf16[8,64,768]{2,1,0:T(8,128)(2,1)S(1)}, bf16[8,64,768]{2,1,0:T(8,128)(2,1)}, u32[]{:S(2)}) copy-start(bf16[8,64,768]{2,1,0:T(8,128)(2,1)} %get-tuple-element.100) | copy-start | bytes 2359300
  262.3 8.0 %copy-start.3 = (f32[24,2304]{1,0:T(8,128)S(1)}, f32[24,2304]{1,0:T(8,128)}, u32[]{:S(2)}) copy-start(f32[24,2304]{1,0:T(8,128)} %get-tuple-element.104) | copy-start | bytes 663556
  262.3 8.7 %copy-start.4 = (f32[24,768]{1,0:T(8,128)S(1)}, f32[24,768]{1,0:T(8,128)}, u32[]{:S(2)}) copy-start(f32[24,768]{1,0:T(8,128)} %get-tuple-element.107) | copy-start | bytes 221188
  262.3 9.3 %copy-start.2 = (f32[24,3072]{1,0:T(8,128)S(1)}, f32[24,3072]{1,0:T(8,128)}, u32[]{:S(2)}) copy-start(f32[24,3072]{1,0:T(8,128)} %get-tuple-element.111) | copy-start | bytes 884740
  262.4 10.1 %copy-start.1 = (f32[96,768]{1,0:T(8,128)S(1)}, f32[96,768]{1,0:T(8,128)}, u32[]{:S(2)}) copy-start(f32[96,768]{1,0:T(8,128)} %get-tuple-element.113) | copy-start | bytes 884740
